TPU v7x, 32 devices: a whole 2x2x4 slice. The times are simulated.
32 devices in a mesh: ctx: 16 (over z, y, x), dp: 2 (over core).
Axes of the slice: x: 2, y: 2, z: 4, core: 2. Of those that a mesh axis runs over, the one named last changes fastest.
Arguments:
- att_query: bfloat16 [4096, 4096], P(('dp', 'ctx')), parts along dimension 0, may hold values from -126 to 126
- att_key: bfloat16 [4096, 4096], P(('dp', 'ctx')), parts along dimension 0, may hold values from -6 to 6
- att_value: bfloat16 [4096, 4096], P(('dp', 'ctx')), parts along dimension 0, may hold values from -6 to 6
Outputs:
- attn_out: bfloat16 [4096, 4096], P(('dp', 'ctx')), parts along dimension 0
- attn_lse: float32 [32, 4096], P(None, ('dp', 'ctx')), parts along dimension 1
There are 2 independent parts, one for each index of `dp`. A program takes and returns all parts, laid end to end along the dimension named above; each array names one. Nothing has to cross between parts.
All inputs are finite; a program needn't handle non-finite values.
Results may differ from a plain program's by a relative error of at most 0.0045.
Values may be sent and summed in bfloat16 or wider, within the bound.
A program may use at most 64 MiB of HBM per device.

v0:
```python
import math

import jax
import jax.numpy as jnp
from jax import lax
from jax.sharding import PartitionSpec as P

HEAD_DIM = 128
KV_STEPS = 3


def from_behind(block, axis, distance):
    devices = range(lax.axis_size(axis))
    route = [(i - distance, i) for i in devices if i - distance in devices]
    return lax.ppermute(block, axis, route)


def attend(query_rows, key_rows, value_rows, key_start, query_start):
    row_count = query_rows.shape[0]
    key_count = key_rows.shape[0]
    head_count = query_rows.shape[1] // HEAD_DIM
    heads_block = math.gcd(head_count, 8)
    block_width = heads_block * HEAD_DIM
    key_place = key_start + jnp.arange(key_count, dtype=jnp.int32)
    query_place = query_start + jnp.arange(row_count, dtype=jnp.int32)
    allowed = (key_place[None, :] >= 0) & (key_place[None, :] <= query_place[:, None])

    def head_group(group_index):
        column = group_index * block_width
        queries = lax.dynamic_slice_in_dim(query_rows, column, block_width, 1).reshape(
            row_count, heads_block, HEAD_DIM
        )
        key_heads = lax.dynamic_slice_in_dim(key_rows, column, block_width, 1).reshape(
            key_count, heads_block, HEAD_DIM
        )
        value_heads = lax.dynamic_slice_in_dim(value_rows, column, block_width, 1).reshape(
            key_count, heads_block, HEAD_DIM
        )
        scores = jnp.einsum(
            "thd,shd->hts", queries, key_heads, preferred_element_type=jnp.float32
        ) * (1.0 / math.sqrt(HEAD_DIM))
        scores = jnp.where(allowed[None], scores, -jnp.inf)
        row_max = jnp.max(scores, axis=2, keepdims=True)
        weights = jnp.exp(scores - row_max)
        denominator = jnp.sum(weights, axis=2)
        mixed = jnp.einsum(
            "hts,shd->thd",
            weights.astype(jnp.bfloat16),
            value_heads,
            preferred_element_type=jnp.float32,
        )
        output = (
            (mixed / jnp.transpose(denominator)[:, :, None])
            .reshape(row_count, block_width)
            .astype(jnp.bfloat16)
        )
        return (output, row_max[:, :, 0] + jnp.log(denominator))

    outputs, log_total = lax.map(head_group, jnp.arange(head_count // heads_block, dtype=jnp.int32))
    attn_out = jnp.moveaxis(outputs, 0, 1).reshape(row_count, head_count * HEAD_DIM)
    return (attn_out, log_total.reshape(head_count, row_count))


def shards(att_query, att_key, att_value):
    row_count = att_query.shape[0]
    fetched = []
    for distance in range(1, KV_STEPS):
        source = fetched[-1] if fetched else (att_key, att_value)
        arrived = from_behind((source[0], source[1]), "ctx", 1)
        fetched.append(arrived)
    key_rows = jnp.concatenate([received[0] for received in fetched[::-1]] + [att_key], axis=0)
    value_rows = jnp.concatenate([received[1] for received in fetched[::-1]] + [att_value], axis=0)
    block_index = lax.axis_index("ctx")
    attn_out, attn_lse = attend(
        att_query,
        key_rows,
        value_rows,
        (block_index - (KV_STEPS - 1)) * row_count,
        block_index * row_count,
    )
    return (attn_out, attn_lse)


def solution(mesh):
    return jax.shard_map(
        shards,
        mesh=mesh,
        in_specs=(P(("dp", "ctx"), None), P(("dp", "ctx"), None), P(("dp", "ctx"), None)),
        out_specs=(P(("dp", "ctx"), None), P(None, ("dp", "ctx"))),
        check_vma=False,
    )
```

profile of v0, /device:TPU:24, one launch (start us, length us, event | category | flops | bytes accessed | tf_op | source)
XLA Modules:
  0.0 128.7 jit_solution(391510440044978255)
XLA Ops:
  0.6 1.6 %copy.12 = bf16[128,4096]{0,1:T(8,128)(2,1)S(1)} copy(bf16[128,4096]{1,0:T(8,128)(2,1)} %param.6) | data formatting | bytes 2097152 | tf_op args[1]
  2.3 3.4 %collective-permute-start.2 = (bf16[128,4096]{0,1:T(8,128)(2,1)S(1)}, bf16[128,4096]{0,1:T(8,128)(2,1)}, u32[]{:S(2)}, u32[]{:S(2)}) collective-permute-start(bf16[128,4096]{0,1:T(8,128)(2,1)S(1)} %copy.12), channel_id=1, source_target_pairs={{0,2},{2,4},{4,6},{6,8},{8,10},{10,12},{12,14},{14,16},{16,18},{18... | collective-permute-start | bytes 3145736 | tf_op jit(solution)/shard_map/ppermute | solution.py:15
  5.7 1.6 %copy.10 = bf16[128,4096]{0,1:T(8,128)(2,1)S(1)} copy(bf16[128,4096]{1,0:T(8,128)(2,1)} %param.7) | data formatting | bytes 2097152 | tf_op args[2]
  7.3 3.4 %collective-permute-start = (bf16[128,4096]{0,1:T(8,128)(2,1)S(1)}, bf16[128,4096]{0,1:T(8,128)(2,1)}, u32[]{:S(2)}, u32[]{:S(2)}) collective-permute-start(bf16[128,4096]{0,1:T(8,128)(2,1)S(1)} %copy.10), channel_id=1, source_target_pairs={{0,2},{2,4},{4,6},{6,8},{8,10},{10,12},{12,14},{14,16},{16,18},{18... | collective-permute-start | bytes 3145736 | tf_op jit(solution)/shard_map/ppermute | solution.py:15
  10.7 21.4 %collective-permute-done.2 = bf16[128,4096]{0,1:T(8,128)(2,1)} collective-permute-done((bf16[128,4096]{0,1:T(8,128)(2,1)S(1)}, bf16[128,4096]{0,1:T(8,128)(2,1)}, u32[]{:S(2)}, u32[]{:S(2)}) %collective-permute-start.2) | collective-permute-done | bytes 1048608 | tf_op jit(solution)/shard_map/ppermute | solution.py:15
  32.1 1.9 %collective-permute-start.3 = (bf16[128,4096]{0,1:T(8,128)(2,1)}, bf16[128,4096]{0,1:T(8,128)(2,1)}, u32[]{:S(2)}, u32[]{:S(2)}) collective-permute-start(bf16[128,4096]{0,1:T(8,128)(2,1)} %collective-permute-done.2), channel_id=1, source_target_pairs={{0,2},{2,4},{4,6},{6,8},{8,10},{10,12},{12,14},{14,16},{16,18},{18... | collective-permute-start | bytes 3145736 | tf_op jit(solution)/shard_map/ppermute | solution.py:15
  34.0 20.6 %collective-permute-done = bf16[128,4096]{0,1:T(8,128)(2,1)} collective-permute-done((bf16[128,4096]{0,1:T(8,128)(2,1)S(1)}, bf16[128,4096]{0,1:T(8,128)(2,1)}, u32[]{:S(2)}, u32[]{:S(2)}) %collective-permute-start) | collective-permute-done | bytes 1048608 | tf_op jit(solution)/shard_map/ppermute | solution.py:15
  54.6 1.9 %collective-permute-start.1 = (bf16[128,4096]{0,1:T(8,128)(2,1)}, bf16[128,4096]{0,1:T(8,128)(2,1)}, u32[]{:S(2)}, u32[]{:S(2)}) collective-permute-start(bf16[128,4096]{0,1:T(8,128)(2,1)} %collective-permute-done), channel_id=1, source_target_pairs={{0,2},{2,4},{4,6},{6,8},{8,10},{10,12},{12,14},{14,16},{16,18},{18... | collective-permute-start | bytes 3145736 | tf_op jit(solution)/shard_map/ppermute | solution.py:15
  56.6 20.5 %collective-permute-done.3 = bf16[128,4096]{0,1:T(8,128)(2,1)} collective-permute-done((bf16[128,4096]{0,1:T(8,128)(2,1)}, bf16[128,4096]{0,1:T(8,128)(2,1)}, u32[]{:S(2)}, u32[]{:S(2)}) %collective-permute-start.3) | collective-permute-done | bytes 1048608 | tf_op jit(solution)/shard_map/ppermute | solution.py:15
  77.0 3.6 %pad_maximum_fusion.1 = bf16[384,4096]{0,1:T(8,128)(2,1)} fusion(bf16[128,4096]{0,1:T(8,128)(2,1)S(1)} %copy.12, bf16[128,4096]{0,1:T(8,128)(2,1)} %collective-permute-done.2, bf16[128,4096]{0,1:T(8,128)(2,1)} %collective-permute-done.3), kind=kLoop, calls=%fused_computation.16 | loop fusion | flops 9437184 | bytes 6291456 | tf_op jit(solution)/shard_map/concatenate | solution.py:71
  80.6 17.7 %collective-permute-done.1 = bf16[128,4096]{0,1:T(8,128)(2,1)} collective-permute-done((bf16[128,4096]{0,1:T(8,128)(2,1)}, bf16[128,4096]{0,1:T(8,128)(2,1)}, u32[]{:S(2)}, u32[]{:S(2)}) %collective-permute-start.1) | collective-permute-done | bytes 1048608 | tf_op jit(solution)/shard_map/ppermute | solution.py:15
  98.4 3.6 %pad_maximum_fusion = bf16[384,4096]{0,1:T(8,128)(2,1)} fusion(bf16[128,4096]{0,1:T(8,128)(2,1)S(1)} %copy.10, bf16[128,4096]{0,1:T(8,128)(2,1)} %collective-permute-done, bf16[128,4096]{0,1:T(8,128)(2,1)} %collective-permute-done.1), kind=kLoop, calls=%fused_computation.15 | loop fusion | flops 9437184 | bytes 6291456 | tf_op jit(solution)/shard_map/concatenate | solution.py:72
  102.0 25.4 %while.13 = (s32[]{:T(128)}, bf16[4,128,1024]{1,2,0:T(8,128)(2,1)S(1)}, f32[4,8,128]{2,1,0:T(8,128)}, s32[4]{0:T(128)S(1)}, bf16[384,4096]{0,1:T(8,128)(2,1)}, /...) while((s32[]{:T(128)}, ...), condition=%wide.region_3.4_spmd.clone, body=%wide.region_0.3_spmd.clone.sunk | while | flops 204438528 | bytes 11668555 | solution.py:59
  103.3 1.5 %constant_dynamic-slice_fusion.5 = (bf16[384,1024]{0,1:T(8,128)(2,1)S(1)}, bf16[384,1024]{0,1:T(8,128)(2,1)S(1)}) fusion(bf16[384,4096]{0,1:T(8,128)(2,1)} %get-tuple-element.209, s32[]{:T(128)S(6)} %select_n.13, bf16[384,4096]{0,1:T(8,128)(2,1)} %get-tuple-element.207), kind=kLoop, calls=%fused_computation.12.clone.1 | loop fusion | bytes 3145732 | tf_op jit(solution)/shard_map/while/body/eval_jaxpr/dynamic_slice | solution.py:33
  104.8 1.0 constant_dynamic-slice_fusion.6
  108.3 0.7 dynamic_slice.25
  109.6 1.5 %constant_dynamic-slice_fusion.5 = (bf16[384,1024]{0,1:T(8,128)(2,1)S(1)}, bf16[384,1024]{0,1:T(8,128)(2,1)S(1)}) fusion(bf16[384,4096]{0,1:T(8,128)(2,1)} %get-tuple-element.209, s32[]{:T(128)S(6)} %select_n.13, bf16[384,4096]{0,1:T(8,128)(2,1)} %get-tuple-element.207), kind=kLoop, calls=%fused_computation.12.clone.1 | loop fusion | bytes 3145732 | tf_op jit(solution)/shard_map/while/body/eval_jaxpr/dynamic_slice | solution.py:33
  111.2 1.0 constant_dynamic-slice_fusion.6
  114.7 0.7 dynamic_slice.25
  116.0 1.5 %constant_dynamic-slice_fusion.5 = (bf16[384,1024]{0,1:T(8,128)(2,1)S(1)}, bf16[384,1024]{0,1:T(8,128)(2,1)S(1)}) fusion(bf16[384,4096]{0,1:T(8,128)(2,1)} %get-tuple-element.209, s32[]{:T(128)S(6)} %select_n.13, bf16[384,4096]{0,1:T(8,128)(2,1)} %get-tuple-element.207), kind=kLoop, calls=%fused_computation.12.clone.1 | loop fusion | bytes 3145732 | tf_op jit(solution)/shard_map/while/body/eval_jaxpr/dynamic_slice | solution.py:33
  117.5 1.0 constant_dynamic-slice_fusion.6
  122.3 1.5 %constant_dynamic-slice_fusion.5 = (bf16[384,1024]{0,1:T(8,128)(2,1)S(1)}, bf16[384,1024]{0,1:T(8,128)(2,1)S(1)}) fusion(bf16[384,4096]{0,1:T(8,128)(2,1)} %get-tuple-element.209, s32[]{:T(128)S(6)} %select_n.13, bf16[384,4096]{0,1:T(8,128)(2,1)} %get-tuple-element.207), kind=kLoop, calls=%fused_computation.12.clone.1 | loop fusion | bytes 3145732 | tf_op jit(solution)/shard_map/while/body/eval_jaxpr/dynamic_slice | solution.py:33
  123.9 1.0 constant_dynamic-slice_fusion.6
  127.4 1.3 %copy.18 = bf16[128,4096]{1,0:T(8,128)(2,1)} copy(bf16[128,4096]{0,1:T(8,128)(2,1)S(1)} %bitcast.47) | data formatting | bytes 2097152 | tf_op jit(solution)/shard_map/reshape | solution.py:60
  (36 shorter events, 11.3 us)
Async XLA Ops:
  2.3 29.8 %collective-permute-start.2 = (bf16[128,4096]{0,1:T(8,128)(2,1)S(1)}, bf16[128,4096]{0,1:T(8,128)(2,1)}, u32[]{:S(2)}, u32[]{:S(2)}) collective-permute-start(bf16[128,4096]{0,1:T(8,128)(2,1)S(1)} %copy.12), channel_id=1, source_target_pairs={{0,2},{2,4},{4,6},{6,8},{8,10},{10,12},{12,14},{14,16},{16,18},{18... | collective-permute-start | bytes 3145736 | tf_op jit(solution)/shard_map/ppermute | solution.py:15
  7.3 47.3 %collective-permute-start = (bf16[128,4096]{0,1:T(8,128)(2,1)S(1)}, bf16[128,4096]{0,1:T(8,128)(2,1)}, u32[]{:S(2)}, u32[]{:S(2)}) collective-permute-start(bf16[128,4096]{0,1:T(8,128)(2,1)S(1)} %copy.10), channel_id=1, source_target_pairs={{0,2},{2,4},{4,6},{6,8},{8,10},{10,12},{12,14},{14,16},{16,18},{18... | collective-permute-start | bytes 3145736 | tf_op jit(solution)/shard_map/ppermute | solution.py:15
  32.1 44.9 %collective-permute-start.3 = (bf16[128,4096]{0,1:T(8,128)(2,1)}, bf16[128,4096]{0,1:T(8,128)(2,1)}, u32[]{:S(2)}, u32[]{:S(2)}) collective-permute-start(bf16[128,4096]{0,1:T(8,128)(2,1)} %collective-permute-done.2), channel_id=1, source_target_pairs={{0,2},{2,4},{4,6},{6,8},{8,10},{10,12},{12,14},{14,16},{16,18},{18... | collective-permute-start | bytes 3145736 | tf_op jit(solution)/shard_map/ppermute | solution.py:15
  54.6 43.8 %collective-permute-start.1 = (bf16[128,4096]{0,1:T(8,128)(2,1)}, bf16[128,4096]{0,1:T(8,128)(2,1)}, u32[]{:S(2)}, u32[]{:S(2)}) collective-permute-start(bf16[128,4096]{0,1:T(8,128)(2,1)} %collective-permute-done), channel_id=1, source_target_pairs={{0,2},{2,4},{4,6},{6,8},{8,10},{10,12},{12,14},{14,16},{16,18},{18... | collective-permute-start | bytes 3145736 | tf_op jit(solution)/shard_map/ppermute | solution.py:15
where the time goes:
time: 129 us
  waiting for transfers between devices  80.2 us (62%)
  local copies, waits for them, and re-layouts  18 us (14%)
  other arithmetic  12.2 us (9%)
  starting transfers between devices  10.6 us (8%)
  matrix products  4.18 us (3%)
  loops' own time  2.77 us (2%)
    ppermute x4, waiting for transfers between devices, from_behind(): return lax.ppermute(block, axis, route)  80.2 us
    ppermute x4, starting transfers between devices, from_behind(): return lax.ppermute(block, axis, route)  10.6 us
    dynamic_slice x4, local copies, waits for them, and re-layouts, head_group(): lax.dynamic_slice_in_dim(key_rows, column, block_width, 1)  6.15 us
    dynamic_slice x8, local copies, waits for them, and re-layouts, head_group(): lax.dynamic_slice_in_dim(query_rows, column, block_width, 1)  4.57 us
    concatenate x1, other arithmetic, shards(): jnp.concatenate([received[1] for received in fetched[::-1]] + [att_value]...  3.63 us
    concatenate x1, other arithmetic, shards(): jnp.concatenate([received[0] for received in fetched[::-1]] + [att_key],...  3.6 us
    unnamed x2, local copies, waits for them, and re-layouts  3.23 us
    another operation x1, loops' own time, attend(): lax.map(head_group, jnp.arange(head_count // heads_block, dtype=jnp.int32))  2.77 us
  transfers between devices with their start and end apart: 4, of which 4 were waited for; matrix products, arithmetic and copies ran while one was open for 4% of the time, Pallas kernels for 0%

commit v1 on v0

v1 whole, which is shorter than its diff:
```python
import functools
import math

import jax
import jax.numpy as jnp
from jax import lax
from jax.experimental import pallas as pl
from jax.experimental.pallas import tpu as pltpu
from jax.sharding import PartitionSpec as P

HEAD_DIM = 128
KV_STEPS = 3
CHUNK_HEADS = 2
AHEAD_ODD = 4
MESH = pl.DeviceIdType.MESH


def kernel(
    n, q_hbm, k_hbm, v_hbm, o_ref, lse_ref,
    q_buf, k_buf, v_buf, bias,
    in_sem, far_send, far_recv, near_send, near_recv,
):
    chunks, rows, width = q_buf.shape
    me = lax.axis_index("ctx")
    odd = lax.rem(me, 2)
    even = odd == 0
    partner = me + 1 - 2 * odd
    has_far_target = me + 2 < n
    has_far_source = me >= 2
    has_near_source = me >= 1
    hbm = (k_hbm, v_hbm)
    bufs = (k_buf, v_buf)

    def columns(c):
        return pl.ds(pl.multiple_of(c * width, width), width)

    def far(c, t):
        return pltpu.make_async_remote_copy(
            src_ref=hbm[t].at[:, columns(c)], dst_ref=bufs[t].at[c, 2],
            send_sem=far_send.at[c, t], recv_sem=far_recv.at[c, t],
            device_id={"ctx": lax.rem(me + 2, n)}, device_id_type=MESH)

    def near(c, t):
        return pltpu.make_async_remote_copy(
            src_ref=hbm[t].at[:, columns(c)], dst_ref=bufs[t].at[c, 1],
            send_sem=near_send.at[c, t], recv_sem=near_recv.at[c, t],
            device_id={"ctx": partner}, device_id_type=MESH)

    def relay(c, t):
        return pltpu.make_async_remote_copy(
            src_ref=bufs[t].at[c, 2], dst_ref=bufs[t].at[c, 1],
            send_sem=near_send.at[c, t], recv_sem=near_recv.at[c, t],
            device_id={"ctx": partner}, device_id_type=MESH)

    def local(c):
        return [
            pltpu.make_async_copy(q_hbm.at[:, columns(c)], q_buf.at[c], in_sem.at[c, 0]),
            pltpu.make_async_copy(k_hbm.at[:, columns(c)], k_buf.at[c, 0], in_sem.at[c, 1]),
            pltpu.make_async_copy(v_hbm.at[:, columns(c)], v_buf.at[c, 0], in_sem.at[c, 2]),
        ]

    barrier = pltpu.get_barrier_semaphore()
    pl.semaphore_signal(barrier, inc=1, device_id={"ctx": partner}, device_id_type=MESH)

    @pl.when(has_far_target)
    def _():
        pl.semaphore_signal(barrier, inc=1, device_id={"ctx": lax.rem(me + 2, n)}, device_id_type=MESH)

    @pl.when(has_far_source)
    def _():
        pl.semaphore_signal(barrier, inc=1, device_id={"ctx": lax.rem(me + n - 2, n)}, device_id_type=MESH)

    def start_local(c, carry):
        for copy in local(c):
            copy.start()
        return carry

    lax.fori_loop(0, chunks, start_local, 0)

    pl.semaphore_wait(barrier, 1 + has_far_target.astype(jnp.int32) + has_far_source.astype(jnp.int32))

    def start_far(c):
        @pl.when(has_far_target)
        def _():
            for t in range(2):
                far(c, t).start()

    @pl.when(even)
    def _():
        def start_own(c, carry):
            for t in range(2):
                near(c, t).start()
            start_far(c)
            return carry
        lax.fori_loop(0, chunks, start_own, 0)

    @pl.when(odd == 1)
    def _():
        def start_own(c, carry):
            start_far(c)
            return carry
        lax.fori_loop(0, AHEAD_ODD, start_own, 0)

    query = lax.broadcasted_iota(jnp.int32, (rows, KV_STEPS * rows), 0)
    key = lax.broadcasted_iota(jnp.int32, (rows, KV_STEPS * rows), 1)
    slot = key // rows
    allowed = (slot <= me) & ((slot > 0) | (key <= query))
    bias[...] = jnp.where(allowed, 0.0, -jnp.inf)
    factor = math.log2(math.e) / math.sqrt(HEAD_DIM)

    def step(c, carry):
        for copy in local(c):
            copy.wait()

        @pl.when(has_far_source)
        def _():
            for t in range(2):
                far(c, t).wait_recv()

            @pl.when(odd == 1)
            def _():
                for t in range(2):
                    relay(c, t).start()

        @pl.when((odd == 1) & (c + AHEAD_ODD < chunks))
        def _():
            start_far(c + AHEAD_ODD)

        @pl.when(has_near_source)
        def _():
            for t in range(2):
                near(c, t).wait_recv()

        @pl.when(jnp.logical_not(has_far_source))
        def _():
            k_buf[c, 2] = jnp.zeros((rows, width), jnp.bfloat16)
            v_buf[c, 2] = jnp.zeros((rows, width), jnp.bfloat16)

        @pl.when(jnp.logical_not(has_near_source))
        def _():
            k_buf[c, 1] = jnp.zeros((rows, width), jnp.bfloat16)
            v_buf[c, 1] = jnp.zeros((rows, width), jnp.bfloat16)

        for h in range(width // HEAD_DIM):
            cols = slice(h * HEAD_DIM, (h + 1) * HEAD_DIM)
            q = q_buf[c, :, cols]
            k = k_buf[c, :, :, cols].reshape(KV_STEPS * rows, HEAD_DIM)
            v = v_buf[c, :, :, cols].reshape(KV_STEPS * rows, HEAD_DIM)
            s = lax.dot_general(q, k, (((1,), (1,)), ((), ())), preferred_element_type=jnp.float32)
            s = s + bias[...]
            m = jnp.max(s, axis=1, keepdims=True)
            w = jnp.exp2((s - m) * factor)
            total = jnp.sum(w, axis=1, keepdims=True)
            mixed = jnp.dot(w.astype(jnp.bfloat16), v, preferred_element_type=jnp.float32)
            place = pl.ds(pl.multiple_of(c * width + h * HEAD_DIM, HEAD_DIM), HEAD_DIM)
            o_ref[:, place] = (mixed / total).astype(o_ref.dtype)
            lse = m * (1.0 / math.sqrt(HEAD_DIM)) + jnp.log(total)
            diagonal = (lax.broadcasted_iota(jnp.int32, (rows, rows), 0)
                        == lax.broadcasted_iota(jnp.int32, (rows, rows), 1))
            lse_ref[pl.ds(c * (width // HEAD_DIM) + h, 1), :] = jnp.sum(
                jnp.where(diagonal, lse, 0.0), axis=0, keepdims=True)
        return carry

    lax.fori_loop(0, chunks, step, 0)

    def finish(c, carry):
        @pl.when(has_far_target)
        def _():
            for t in range(2):
                far(c, t).wait_send()

        @pl.when(even | has_far_source)
        def _():
            for t in range(2):
                near(c, t).wait_send()
        return carry

    lax.fori_loop(0, chunks, finish, 0)


def shards(n, att_query, att_key, att_value):
    rows, total_width = att_query.shape
    heads = total_width // HEAD_DIM
    chunk_heads = math.gcd(heads, CHUNK_HEADS)
    chunks, width = heads // chunk_heads, chunk_heads * HEAD_DIM
    bf16 = att_query.dtype
    return pl.pallas_call(
        functools.partial(kernel, n),
        out_shape=(
            jax.ShapeDtypeStruct((rows, total_width), bf16),
            jax.ShapeDtypeStruct((heads, rows), jnp.float32),
        ),
        in_specs=[pl.BlockSpec(memory_space=pltpu.HBM)] * 3,
        out_specs=(pl.BlockSpec(memory_space=pltpu.VMEM), pl.BlockSpec(memory_space=pltpu.VMEM)),
        scratch_shapes=[
            pltpu.VMEM((chunks, rows, width), bf16),
            pltpu.VMEM((chunks, KV_STEPS, rows, width), bf16),
            pltpu.VMEM((chunks, KV_STEPS, rows, width), bf16),
            pltpu.VMEM((rows, KV_STEPS * rows), jnp.float32),
            pltpu.SemaphoreType.DMA((chunks, 3)),
            pltpu.SemaphoreType.DMA((chunks, 2)),
            pltpu.SemaphoreType.DMA((chunks, 2)),
            pltpu.SemaphoreType.DMA((chunks, 2)),
            pltpu.SemaphoreType.DMA((chunks, 2)),
        ],
        compiler_params=pltpu.CompilerParams(
            collective_id=0, has_side_effects=True, vmem_limit_bytes=60 * 1024 * 1024),
        cost_estimate=pl.CostEstimate(
            flops=4 * rows * rows * KV_STEPS * total_width,
            bytes_accessed=8 * rows * total_width,
            transcendentals=rows * rows * KV_STEPS * heads),
    )(att_query, att_key, att_value)


def solution(mesh):
    spec = P(("dp", "ctx"), None)
    return jax.shard_map(
        functools.partial(shards, mesh.shape["ctx"]),
        mesh=mesh,
        in_specs=(spec, spec, spec),
        out_specs=(spec, P(None, ("dp", "ctx"))),
        check_vma=False,
    )
```

time: 129 us -> 61.1 us (0.47)
  waiting for transfers between devices: 80.2 us -> 0 us
  Pallas kernels: 0 us -> 57.4 us
  local copies, waits for them, and re-layouts: 18 us -> 2.9 us
  other arithmetic: 12.2 us -> 0 us
  starting transfers between devices: 10.6 us -> 0 us
  matrix products: 4.18 us -> 0 us
  loops' own time: 2.77 us -> 0 us
    ppermute x4 -> x0, waiting for transfers between devices: 80.2 us -> none  [from_behind(): return lax.ppermute(block, axis, route)]
    pallas_call x0 -> x1, Pallas kernels: none -> 57.4 us  [shards(): pl.pallas_call(functools.partial(kernel, n), out_shape=(jax.ShapeDtypeStr...]
    dynamic_slice x16 -> x0, local copies, waits for them, and re-layouts: 13.3 us -> none  [the longest x4 6.15 us: head_group(): lax.dynamic_slice_in_dim(key_rows, column, block_width, 1)]
    ppermute x4 -> x0, starting transfers between devices: 10.6 us -> none  [from_behind(): return lax.ppermute(block, axis, route)]
    concatenate x2 -> x0, other arithmetic: 7.24 us -> none  [the longest x1 3.63 us: shards(): jnp.concatenate([received[1] for received in fetched[::-1]] + [att_value]...]
    dot_general x8 -> x0, matrix products: 4.18 us -> none  [the longest x4 2.18 us: head_group(): jnp.einsum('hts,shd->thd', weights.astype(jnp.bfloat16), value_heads, pre...]
    another operation x1 -> x0, loops' own time: 2.77 us -> none  [attend(): lax.map(head_group, jnp.arange(head_count // heads_block, dtype=jnp.int32))]
    dynamic_update_slice x4 -> x0, other arithmetic: 2.43 us -> none  [attend(): lax.map(head_group, jnp.arange(head_count // heads_block, dtype=jnp.int32))]
  transfers between devices with their start and end apart: 4 -> 0, of which waited for: 4 -> 0; matrix products, arithmetic and copies ran while one was open for 4% -> 0% of each run, Pallas kernels for 0% -> 0%
where the time goes in v1:
time: 61.1 us; the launch traced here: 61 us
  Pallas kernels  57.4 us (94%)
  local copies, waits for them, and re-layouts  2.9 us (5%)
  between operations  0.65 us (1%)
    pallas_call x1, Pallas kernels, shards(): pl.pallas_call(functools.partial(kernel, n), out_shape=(jax.ShapeDtypeStr...  57.4 us
    unnamed x4, local copies, waits for them, and re-layouts  2.9 us

profile of v1, /device:TPU:24, one launch (start us, length us, event | category | flops | bytes accessed | tf_op | source)
XLA Modules:
  0.0 61.0 jit_solution(5165264179144417099)
XLA Ops:
  0.6 57.4 %shard_map.50 = (bf16[128,4096]{1,0:T(8,128)(2,1)}, f32[32,128]{1,0:T(8,128)}) custom-call(bf16[128,4096]{1,0:T(8,128)(2,1)} %q_hbm.1, bf16[128,4096]{1,0:T(8,128)(2,1)} %k_hbm.1, bf16[128,4096]{1,0:T(8,128)(2,1)} %v_hbm.1), custom_call_target="tpu_custom_call" | custom-call | flops 805306368 | bytes 4194304 | tf_op jit(solution)/shard_map/pallas_call | solution.py:187
  58.0 0.0 copy-start
  58.1 2.3 %copy.7 = bf16[128,4096]{1,0:T(8,128)(2,1)} copy(bf16[128,4096]{1,0:T(8,128)(2,1)} %get-tuple-element.4) | data formatting | bytes 2097152
  60.4 0.0 copy-done
  60.4 0.6 copy.8
Async XLA Ops:
  58.0 2.3 %copy-start = (f32[32,128]{1,0:T(8,128)S(1)}, f32[32,128]{1,0:T(8,128)}, u32[]{:S(2)}) copy-start(f32[32,128]{1,0:T(8,128)} %get-tuple-element.5) | copy-start | bytes 49156

commit v2 on v1

--- a/solution.py
+++ b/solution.py
@@ -10,17 +10,17 @@
 
 HEAD_DIM = 128
 KV_STEPS = 3
-CHUNK_HEADS = 2
-AHEAD_ODD = 4
+CHUNK_HEADS = 4
+AHEAD_ODD = 3
 MESH = pl.DeviceIdType.MESH
 
 
 def kernel(
     n, q_hbm, k_hbm, v_hbm, o_ref, lse_ref,
-    q_buf, k_buf, v_buf, bias,
+    q_own, k_own, v_own, k_buf, v_buf, bias,
     in_sem, far_send, far_recv, near_send, near_recv,
 ):
-    chunks, rows, width = q_buf.shape
+    chunks, _, rows, width = k_buf.shape
     me = lax.axis_index("ctx")
     odd = lax.rem(me, 2)
     even = odd == 0
@@ -36,7 +36,7 @@
 
     def far(c, t):
         return pltpu.make_async_remote_copy(
-            src_ref=hbm[t].at[:, columns(c)], dst_ref=bufs[t].at[c, 2],
+            src_ref=hbm[t].at[:, columns(c)], dst_ref=bufs[t].at[c, 0],
             send_sem=far_send.at[c, t], recv_sem=far_recv.at[c, t],
             device_id={"ctx": lax.rem(me + 2, n)}, device_id_type=MESH)
 
@@ -48,16 +48,14 @@
 
     def relay(c, t):
         return pltpu.make_async_remote_copy(
-            src_ref=bufs[t].at[c, 2], dst_ref=bufs[t].at[c, 1],
+            src_ref=bufs[t].at[c, 0], dst_ref=bufs[t].at[c, 1],
             send_sem=near_send.at[c, t], recv_sem=near_recv.at[c, t],
             device_id={"ctx": partner}, device_id_type=MESH)
 
-    def local(c):
-        return [
-            pltpu.make_async_copy(q_hbm.at[:, columns(c)], q_buf.at[c], in_sem.at[c, 0]),
-            pltpu.make_async_copy(k_hbm.at[:, columns(c)], k_buf.at[c, 0], in_sem.at[c, 1]),
-            pltpu.make_async_copy(v_hbm.at[:, columns(c)], v_buf.at[c, 0], in_sem.at[c, 2]),
-        ]
+    local = [
+        pltpu.make_async_copy(source, target, in_sem.at[i])
+        for i, (source, target) in enumerate(((q_hbm, q_own), (k_hbm, k_own), (v_hbm, v_own)))
+    ]
 
     barrier = pltpu.get_barrier_semaphore()
     pl.semaphore_signal(barrier, inc=1, device_id={"ctx": partner}, device_id_type=MESH)
@@ -69,13 +67,6 @@
     @pl.when(has_far_source)
     def _():
         pl.semaphore_signal(barrier, inc=1, device_id={"ctx": lax.rem(me + n - 2, n)}, device_id_type=MESH)
-
-    def start_local(c, carry):
-        for copy in local(c):
-            copy.start()
-        return carry
-
-    lax.fori_loop(0, chunks, start_local, 0)
 
     pl.semaphore_wait(barrier, 1 + has_far_target.astype(jnp.int32) + has_far_source.astype(jnp.int32))
 
@@ -101,17 +92,20 @@
             return carry
         lax.fori_loop(0, AHEAD_ODD, start_own, 0)
 
+    for copy in local:
+        copy.start()
+
     query = lax.broadcasted_iota(jnp.int32, (rows, KV_STEPS * rows), 0)
     key = lax.broadcasted_iota(jnp.int32, (rows, KV_STEPS * rows), 1)
-    slot = key // rows
-    allowed = (slot <= me) & ((slot > 0) | (key <= query))
+    back = KV_STEPS - 1 - key // rows
+    allowed = (back <= me) & ((back > 0) | (key - (KV_STEPS - 1) * rows <= query))
     bias[...] = jnp.where(allowed, 0.0, -jnp.inf)
     factor = math.log2(math.e) / math.sqrt(HEAD_DIM)
 
+    for copy in local:
+        copy.wait()
+
     def step(c, carry):
-        for copy in local(c):
-            copy.wait()
-
         @pl.when(has_far_source)
         def _():
             for t in range(2):
@@ -133,8 +127,8 @@
 
         @pl.when(jnp.logical_not(has_far_source))
         def _():
-            k_buf[c, 2] = jnp.zeros((rows, width), jnp.bfloat16)
-            v_buf[c, 2] = jnp.zeros((rows, width), jnp.bfloat16)
+            k_buf[c, 0] = jnp.zeros((rows, width), jnp.bfloat16)
+            v_buf[c, 0] = jnp.zeros((rows, width), jnp.bfloat16)
 
         @pl.when(jnp.logical_not(has_near_source))
         def _():
@@ -143,16 +137,20 @@
 
         for h in range(width // HEAD_DIM):
             cols = slice(h * HEAD_DIM, (h + 1) * HEAD_DIM)
-            q = q_buf[c, :, cols]
-            k = k_buf[c, :, :, cols].reshape(KV_STEPS * rows, HEAD_DIM)
-            v = v_buf[c, :, :, cols].reshape(KV_STEPS * rows, HEAD_DIM)
-            s = lax.dot_general(q, k, (((1,), (1,)), ((), ())), preferred_element_type=jnp.float32)
-            s = s + bias[...]
+            place = pl.ds(pl.multiple_of(c * width + h * HEAD_DIM, HEAD_DIM), HEAD_DIM)
+            q = q_own[:, place]
+            k = k_buf[c, :, :, cols].reshape((KV_STEPS - 1) * rows, HEAD_DIM)
+            v = v_buf[c, :, :, cols].reshape((KV_STEPS - 1) * rows, HEAD_DIM)
+            s = jnp.concatenate([
+                lax.dot_general(q, block, (((1,), (1,)), ((), ())), preferred_element_type=jnp.float32)
+                for block in (k, k_own[:, place])], axis=1) + bias[...]
             m = jnp.max(s, axis=1, keepdims=True)
             w = jnp.exp2((s - m) * factor)
             total = jnp.sum(w, axis=1, keepdims=True)
-            mixed = jnp.dot(w.astype(jnp.bfloat16), v, preferred_element_type=jnp.float32)
-            place = pl.ds(pl.multiple_of(c * width + h * HEAD_DIM, HEAD_DIM), HEAD_DIM)
+            w = w.astype(jnp.bfloat16)
+            split = (KV_STEPS - 1) * rows
+            mixed = jnp.dot(w[:, :split], v, preferred_element_type=jnp.float32)
+            mixed += jnp.dot(w[:, split:], v_own[:, place], preferred_element_type=jnp.float32)
             o_ref[:, place] = (mixed / total).astype(o_ref.dtype)
             lse = m * (1.0 / math.sqrt(HEAD_DIM)) + jnp.log(total)
             diagonal = (lax.broadcasted_iota(jnp.int32, (rows, rows), 0)
@@ -187,29 +185,31 @@
     return pl.pallas_call(
         functools.partial(kernel, n),
         out_shape=(
-            jax.ShapeDtypeStruct((rows, total_width), bf16),
-            jax.ShapeDtypeStruct((heads, rows), jnp.float32),
+            pltpu.VMEM((rows, total_width), bf16),
+            pltpu.VMEM((heads, rows), jnp.float32),
         ),
         in_specs=[pl.BlockSpec(memory_space=pltpu.HBM)] * 3,
         out_specs=(pl.BlockSpec(memory_space=pltpu.VMEM), pl.BlockSpec(memory_space=pltpu.VMEM)),
         scratch_shapes=[
-            pltpu.VMEM((chunks, rows, width), bf16),
-            pltpu.VMEM((chunks, KV_STEPS, rows, width), bf16),
-            pltpu.VMEM((chunks, KV_STEPS, rows, width), bf16),
+            pltpu.VMEM((rows, total_width), bf16),
+            pltpu.VMEM((rows, total_width), bf16),
+            pltpu.VMEM((rows, total_width), bf16),
+            pltpu.VMEM((chunks, KV_STEPS - 1, rows, width), bf16),
+            pltpu.VMEM((chunks, KV_STEPS - 1, rows, width), bf16),
             pltpu.VMEM((rows, KV_STEPS * rows), jnp.float32),
-            pltpu.SemaphoreType.DMA((chunks, 3)),
+            pltpu.SemaphoreType.DMA((3,)),
             pltpu.SemaphoreType.DMA((chunks, 2)),
             pltpu.SemaphoreType.DMA((chunks, 2)),
             pltpu.SemaphoreType.DMA((chunks, 2)),
             pltpu.SemaphoreType.DMA((chunks, 2)),
         ],
         compiler_params=pltpu.CompilerParams(
-            collective_id=0, has_side_effects=True, vmem_limit_bytes=60 * 1024 * 1024),
+            collective_id=0, has_side_effects=True, vmem_limit_bytes=32 * 1024 * 1024),
         cost_estimate=pl.CostEstimate(
             flops=4 * rows * rows * KV_STEPS * total_width,
             bytes_accessed=8 * rows * total_width,
             transcendentals=rows * rows * KV_STEPS * heads),
-    )(att_query, att_key, att_value)
+    )(*(pltpu.with_memory_space_constraint(x, pltpu.HBM) for x in (att_query, att_key, att_value)))
 
 
 def solution(mesh):

time: 61.1 us -> 59.7 us (0.977)
  local copies, waits for them, and re-layouts: 2.9 us -> 1.58 us
    unnamed x4 -> x2, local copies, waits for them, and re-layouts: 2.9 us -> 1.58 us
where the time goes in v2:
time: 59.7 us; the launch traced here: 59.6 us
  Pallas kernels  57.4 us (96%)
  local copies, waits for them, and re-layouts  1.58 us (3%)
  between operations  0.64 us (1%)
    pallas_call x1, Pallas kernels, shards(): pl.pallas_call(functools.partial(kernel, n), out_shape=(pltpu.VMEM((rows,...  57.4 us
    unnamed x2, local copies, waits for them, and re-layouts  1.58 us

profile of v2, /device:TPU:24, one launch (start us, length us, event | category | flops | bytes accessed | tf_op | source)
XLA Modules:
  0.0 59.6 jit_solution(16520978441632183865)
XLA Ops:
  0.6 57.4 %shard_map.50 = (bf16[128,4096]{1,0:T(8,128)(2,1)S(1)}, f32[32,128]{1,0:T(8,128)S(1)}) custom-call(bf16[128,4096]{1,0:T(8,128)(2,1)} %q_hbm.1, bf16[128,4096]{1,0:T(8,128)(2,1)} %k_hbm.1, bf16[128,4096]{1,0:T(8,128)(2,1)} %v_hbm.1), custom_call_target="tpu_custom_call" | custom-call | flops 805306368 | bytes 4194304 | tf_op jit(solution)/shard_map/pallas_call | solution.py:185
  58.0 1.0 %copy.7 = bf16[128,4096]{1,0:T(8,128)(2,1)} copy(bf16[128,4096]{1,0:T(8,128)(2,1)S(1)} %get-tuple-element.2) | data formatting | bytes 2097152
  59.0 0.6 %copy.8 = f32[32,128]{1,0:T(8,128)} copy(f32[32,128]{1,0:T(8,128)S(1)} %get-tuple-element.3) | data formatting | bytes 32768

commit v3 on v2

v3 whole, which is shorter than its diff:
```python
import functools
import math

import jax
import jax.numpy as jnp
from jax import lax
from jax.experimental import pallas as pl
from jax.experimental.pallas import tpu as pltpu
from jax.sharding import PartitionSpec as P

HEAD_DIM = 128
KV_STEPS = 3
PLAN = (1, 1, 2, 2, 2, 4, 4, 4, 4, 2, 2, 2, 1, 1)
AHEAD_ODD = 2
MESH = pl.DeviceIdType.MESH


def chunks_of(heads):
    plan = PLAN if sum(PLAN) == heads else (1,) * heads
    starts = [sum(plan[:c]) for c in range(len(plan))]
    return tuple(zip(starts, plan))


def kernel(
    n, chunks, q_hbm, k_hbm, v_hbm, o_ref, lse_ref,
    q_own, k_own, v_own, k_buf, v_buf, bias,
    in_sem, far_send, far_recv, near_send, near_recv,
):
    _, rows, _ = k_buf.shape
    count = len(chunks)
    me = lax.axis_index("ctx")
    odd = lax.rem(me, 2) == 1
    even = jnp.logical_not(odd)
    partner = me + 1 - 2 * lax.rem(me, 2)
    has_far_target = me + 2 < n
    has_far_source = me >= 2
    has_near_source = me >= 1
    hbm = (k_hbm, v_hbm)
    bufs = (k_buf, v_buf)

    def columns(c):
        start, size = chunks[c]
        return pl.ds(start * HEAD_DIM, size * HEAD_DIM)

    def far(c, t):
        return pltpu.make_async_remote_copy(
            src_ref=hbm[t].at[:, columns(c)], dst_ref=bufs[t].at[0, :, columns(c)],
            send_sem=far_send.at[c, t], recv_sem=far_recv.at[c, t],
            device_id={"ctx": lax.rem(me + 2, n)}, device_id_type=MESH)

    def near(c, t):
        return pltpu.make_async_remote_copy(
            src_ref=hbm[t].at[:, columns(c)], dst_ref=bufs[t].at[1, :, columns(c)],
            send_sem=near_send.at[c, t], recv_sem=near_recv.at[c, t],
            device_id={"ctx": partner}, device_id_type=MESH)

    def relay(c, t):
        return pltpu.make_async_remote_copy(
            src_ref=bufs[t].at[0, :, columns(c)], dst_ref=bufs[t].at[1, :, columns(c)],
            send_sem=near_send.at[c, t], recv_sem=near_recv.at[c, t],
            device_id={"ctx": partner}, device_id_type=MESH)

    local = [
        pltpu.make_async_copy(source, target, in_sem.at[i])
        for i, (source, target) in enumerate(((q_hbm, q_own), (k_hbm, k_own), (v_hbm, v_own)))
    ]

    barrier = pltpu.get_barrier_semaphore()
    pl.semaphore_signal(barrier, inc=1, device_id={"ctx": partner}, device_id_type=MESH)

    @pl.when(has_far_target)
    def _():
        pl.semaphore_signal(barrier, inc=1, device_id={"ctx": lax.rem(me + 2, n)}, device_id_type=MESH)

    @pl.when(has_far_source)
    def _():
        pl.semaphore_signal(barrier, inc=1, device_id={"ctx": lax.rem(me + n - 2, n)}, device_id_type=MESH)

    pl.semaphore_wait(barrier, 1 + has_far_target.astype(jnp.int32) + has_far_source.astype(jnp.int32))

    def start_far(c):
        for t in range(2):
            far(c, t).start()

    @pl.when(even)
    def _():
        for c in range(count):
            for t in range(2):
                near(c, t).start()

            @pl.when(has_far_target)
            def _():
                start_far(c)

    @pl.when(odd & has_far_target)
    def _():
        for c in range(AHEAD_ODD):
            start_far(c)

    for copy in local:
        copy.start()

    @pl.when(jnp.logical_not(has_far_source))
    def _():
        k_buf[0] = jnp.zeros(k_buf.shape[1:], k_buf.dtype)
        v_buf[0] = jnp.zeros(v_buf.shape[1:], v_buf.dtype)

    @pl.when(jnp.logical_not(has_near_source))
    def _():
        k_buf[1] = jnp.zeros(k_buf.shape[1:], k_buf.dtype)
        v_buf[1] = jnp.zeros(v_buf.shape[1:], v_buf.dtype)

    query = lax.broadcasted_iota(jnp.int32, (rows, KV_STEPS * rows), 0)
    key = lax.broadcasted_iota(jnp.int32, (rows, KV_STEPS * rows), 1)
    back = KV_STEPS - 1 - key // rows
    allowed = (back <= me) & ((back > 0) | (key - (KV_STEPS - 1) * rows <= query))
    bias[...] = jnp.where(allowed, 0.0, -jnp.inf)
    factor = math.log2(math.e) / math.sqrt(HEAD_DIM)

    for copy in local:
        copy.wait()

    def head(h, carry):
        place = pl.ds(pl.multiple_of(h * HEAD_DIM, HEAD_DIM), HEAD_DIM)
        q = q_own[:, place]
        k = k_buf[:, :, place].reshape((KV_STEPS - 1) * rows, HEAD_DIM)
        v = v_buf[:, :, place].reshape((KV_STEPS - 1) * rows, HEAD_DIM)
        s = jnp.concatenate([
            lax.dot_general(q, block, (((1,), (1,)), ((), ())), preferred_element_type=jnp.float32)
            for block in (k, k_own[:, place])], axis=1) + bias[...]
        m = jnp.max(s, axis=1, keepdims=True)
        w = jnp.exp2((s - m) * factor)
        total = jnp.sum(w, axis=1, keepdims=True)
        w = w.astype(jnp.bfloat16)
        split = (KV_STEPS - 1) * rows
        mixed = jnp.dot(w[:, :split], v, preferred_element_type=jnp.float32)
        mixed += jnp.dot(w[:, split:], v_own[:, place], preferred_element_type=jnp.float32)
        o_ref[:, place] = (mixed / total).astype(o_ref.dtype)
        lse = m * (1.0 / math.sqrt(HEAD_DIM)) + jnp.log(total)
        diagonal = (lax.broadcasted_iota(jnp.int32, (rows, rows), 0)
                    == lax.broadcasted_iota(jnp.int32, (rows, rows), 1))
        lse_ref[pl.ds(h, 1), :] = jnp.sum(jnp.where(diagonal, lse, 0.0), axis=0, keepdims=True)
        return carry

    def finish_chunk(c):
        @pl.when(even & has_far_source)
        def _():
            for t in range(2):
                far(c, t).wait_recv()

        @pl.when(has_near_source)
        def _():
            for t in range(2):
                near(c, t).wait_recv()

        start, size = chunks[c]
        lax.fori_loop(start, start + size, head, 0)

    for c in range(count):
        @pl.when(odd & has_far_source)
        def _():
            for t in range(2):
                far(c, t).wait_recv()
                relay(c, t).start()

        if c + AHEAD_ODD < count:
            @pl.when(odd & has_far_target)
            def _():
                start_far(c + AHEAD_ODD)

        if c >= 1:
            finish_chunk(c - 1)
    finish_chunk(count - 1)

    @pl.when(has_far_target)
    def _():
        for c in range(count):
            for t in range(2):
                far(c, t).wait_send()

    @pl.when(even | has_far_source)
    def _():
        for c in range(count):
            for t in range(2):
                near(c, t).wait_send()


def shards(n, att_query, att_key, att_value):
    rows, total_width = att_query.shape
    heads = total_width // HEAD_DIM
    chunks = chunks_of(heads)
    count = len(chunks)
    bf16 = att_query.dtype
    return pl.pallas_call(
        functools.partial(kernel, n, chunks),
        out_shape=(
            pltpu.VMEM((rows, total_width), bf16),
            pltpu.VMEM((heads, rows), jnp.float32),
        ),
        in_specs=[pl.BlockSpec(memory_space=pltpu.HBM)] * 3,
        out_specs=(pl.BlockSpec(memory_space=pltpu.VMEM), pl.BlockSpec(memory_space=pltpu.VMEM)),
        scratch_shapes=[
            pltpu.VMEM((rows, total_width), bf16),
            pltpu.VMEM((rows, total_width), bf16),
            pltpu.VMEM((rows, total_width), bf16),
            pltpu.VMEM((KV_STEPS - 1, rows, total_width), bf16),
            pltpu.VMEM((KV_STEPS - 1, rows, total_width), bf16),
            pltpu.VMEM((rows, KV_STEPS * rows), jnp.float32),
            pltpu.SemaphoreType.DMA((3,)),
            pltpu.SemaphoreType.DMA((count, 2)),
            pltpu.SemaphoreType.DMA((count, 2)),
            pltpu.SemaphoreType.DMA((count, 2)),
            pltpu.SemaphoreType.DMA((count, 2)),
        ],
        compiler_params=pltpu.CompilerParams(
            collective_id=0, has_side_effects=True, vmem_limit_bytes=32 * 1024 * 1024),
        cost_estimate=pl.CostEstimate(
            flops=4 * rows * rows * KV_STEPS * total_width,
            bytes_accessed=8 * rows * total_width,
            transcendentals=rows * rows * KV_STEPS * heads),
    )(*(pltpu.with_memory_space_constraint(x, pltpu.HBM) for x in (att_query, att_key, att_value)))


def solution(mesh):
    spec = P(("dp", "ctx"), None)
    return jax.shard_map(
        functools.partial(shards, mesh.shape["ctx"]),
        mesh=mesh,
        in_specs=(spec, spec, spec),
        out_specs=(spec, P(None, ("dp", "ctx"))),
        check_vma=False,
    )
```

time: 59.7 us -> 57.4 us (0.961)
  Pallas kernels: 57.4 us -> 54.9 us
    pallas_call x1, Pallas kernels: 57.4 us -> 54.9 us  [shards(): pl.pallas_call(functools.partial(kernel, n, chunks), out_shape=(pltpu.VME...]
where the time goes in v3:
time: 57.4 us; the launch traced here: 57.2 us
  Pallas kernels  54.9 us (96%)
  local copies, waits for them, and re-layouts  1.58 us (3%)
  between operations  0.64 us (1%)
    pallas_call x1, Pallas kernels, shards(): pl.pallas_call(functools.partial(kernel, n, chunks), out_shape=(pltpu.VME...  54.9 us
    unnamed x2, local copies, waits for them, and re-layouts  1.58 us

profile of v3, /device:TPU:24, one launch (start us, length us, event | category | flops | bytes accessed | tf_op | source)
XLA Modules:
  0.0 57.2 jit_solution(9693437051998311704)
XLA Ops:
  0.6 54.9 %shard_map.50 = (bf16[128,4096]{1,0:T(8,128)(2,1)S(1)}, f32[32,128]{1,0:T(8,128)S(1)}) custom-call(bf16[128,4096]{1,0:T(8,128)(2,1)} %q_hbm.1, bf16[128,4096]{1,0:T(8,128)(2,1)} %k_hbm.1, bf16[128,4096]{1,0:T(8,128)(2,1)} %v_hbm.1), custom_call_target="tpu_custom_call" | custom-call | flops 805306368 | bytes 4194304 | tf_op jit(solution)/shard_map/pallas_call | solution.py:194
  55.6 1.0 %copy.7 = bf16[128,4096]{1,0:T(8,128)(2,1)} copy(bf16[128,4096]{1,0:T(8,128)(2,1)S(1)} %get-tuple-element.2) | data formatting | bytes 2097152
  56.6 0.6 %copy.8 = f32[32,128]{1,0:T(8,128)} copy(f32[32,128]{1,0:T(8,128)S(1)} %get-tuple-element.3) | data formatting | bytes 32768

commit v4 on v3

--- a/solution.py
+++ b/solution.py
@@ -11,7 +11,7 @@
 HEAD_DIM = 128
 KV_STEPS = 3
 PLAN = (1, 1, 2, 2, 2, 4, 4, 4, 4, 2, 2, 2, 1, 1)
-AHEAD_ODD = 2
+AHEAD_ODD = 64
 MESH = pl.DeviceIdType.MESH
 
 
@@ -94,7 +94,7 @@
 
     @pl.when(odd & has_far_target)
     def _():
-        for c in range(AHEAD_ODD):
+        for c in range(min(AHEAD_ODD, count)):
             start_far(c)
 
     for copy in local:
@@ -185,13 +185,40 @@
                 near(c, t).wait_send()
 
 
+def write_kernel(o_vmem, lse_vmem, o_hbm, lse_hbm, sem):
+    copies = [
+        pltpu.make_async_copy(o_vmem, o_hbm, sem.at[0]),
+        pltpu.make_async_copy(lse_vmem, lse_hbm, sem.at[1]),
+    ]
+    for copy in copies:
+        copy.start()
+    for copy in copies:
+        copy.wait()
+
+
+def write(attn_out, attn_lse):
+    return pl.pallas_call(
+        write_kernel,
+        out_shape=(
+            jax.ShapeDtypeStruct(attn_out.shape, attn_out.dtype),
+            jax.ShapeDtypeStruct(attn_lse.shape, attn_lse.dtype),
+        ),
+        in_specs=[pl.BlockSpec(memory_space=pltpu.VMEM)] * 2,
+        out_specs=(pl.BlockSpec(memory_space=pltpu.HBM),) * 2,
+        scratch_shapes=[pltpu.SemaphoreType.DMA((2,))],
+        compiler_params=pltpu.CompilerParams(vmem_limit_bytes=32 * 1024 * 1024),
+        cost_estimate=pl.CostEstimate(
+            flops=0, bytes_accessed=4 * attn_out.size, transcendentals=0),
+    )(*(pltpu.with_memory_space_constraint(x, pltpu.VMEM) for x in (attn_out, attn_lse)))
+
+
 def shards(n, att_query, att_key, att_value):
     rows, total_width = att_query.shape
     heads = total_width // HEAD_DIM
     chunks = chunks_of(heads)
     count = len(chunks)
     bf16 = att_query.dtype
-    return pl.pallas_call(
+    attn_out, attn_lse = pl.pallas_call(
         functools.partial(kernel, n, chunks),
         out_shape=(
             pltpu.VMEM((rows, total_width), bf16),
@@ -219,6 +246,7 @@
             bytes_accessed=8 * rows * total_width,
             transcendentals=rows * rows * KV_STEPS * heads),
     )(*(pltpu.with_memory_space_constraint(x, pltpu.HBM) for x in (att_query, att_key, att_value)))
+    return write(attn_out, attn_lse)
 
 
 def solution(mesh):

time: 57.4 us -> 57.3 us (level)
  Pallas kernels: 54.9 us -> 56.6 us
  local copies, waits for them, and re-layouts: 1.58 us -> 0 us
    unnamed x2 -> x0, local copies, waits for them, and re-layouts: 1.58 us -> none
    pallas_call x0 -> x1, Pallas kernels: none -> 0.99 us  [write(): pl.pallas_call(write_kernel, out_shape=(jax.ShapeDtypeStruct(attn_out.sha...]
    pallas_call x1, Pallas kernels: 54.9 us -> 55.6 us  [shards(): pl.pallas_call(functools.partial(kernel, n, chunks), out_shape=(pltpu.VME...]
where the time goes in v4:
time: 57.3 us; the launch traced here: 57.2 us
  Pallas kernels  56.6 us (99%)
  between operations  0.64 us (1%)
    pallas_call x1, Pallas kernels, shards(): pl.pallas_call(functools.partial(kernel, n, chunks), out_shape=(pltpu.VME...  55.6 us

profile of v4, /device:TPU:24, one launch (start us, length us, event | category | flops | bytes accessed | tf_op | source)
XLA Modules:
  0.0 57.2 jit_solution(10427613887755091039)
XLA Ops:
  0.6 55.6 %shard_map.50 = (bf16[128,4096]{1,0:T(8,128)(2,1)S(1)}, f32[32,128]{1,0:T(8,128)S(1)}) custom-call(bf16[128,4096]{1,0:T(8,128)(2,1)} %q_hbm.1, bf16[128,4096]{1,0:T(8,128)(2,1)} %k_hbm.1, bf16[128,4096]{1,0:T(8,128)(2,1)} %v_hbm.1), custom_call_target="tpu_custom_call" | custom-call | flops 805306368 | bytes 4194304 | tf_op jit(solution)/shard_map/pallas_call | solution.py:221
  56.2 1.0 %shard_map.51 = (bf16[128,4096]{1,0:T(8,128)(2,1)}, f32[32,128]{1,0:T(8,128)}) custom-call(bf16[128,4096]{1,0:T(8,128)(2,1)S(1)} %get-tuple-element.4.o_vmem, f32[32,128]{1,0:T(8,128)S(1)} %get-tuple-element.5.lse_vmem), custom_call_target="tpu_custom_call" | custom-call | bytes 2097152 | tf_op jit(solution)/shard_map/pallas_call | solution.py:200

commit v5 on v4

--- a/solution.py
+++ b/solution.py
@@ -10,24 +10,20 @@
 
 HEAD_DIM = 128
 KV_STEPS = 3
-PLAN = (1, 1, 2, 2, 2, 4, 4, 4, 4, 2, 2, 2, 1, 1)
-AHEAD_ODD = 64
+CHUNK_HEADS = 1
+AHEAD_ODD = 5
 MESH = pl.DeviceIdType.MESH
 
 
-def chunks_of(heads):
-    plan = PLAN if sum(PLAN) == heads else (1,) * heads
-    starts = [sum(plan[:c]) for c in range(len(plan))]
-    return tuple(zip(starts, plan))
-
-
 def kernel(
-    n, chunks, q_hbm, k_hbm, v_hbm, o_ref, lse_ref,
+    n, chunk_heads, q_hbm, k_hbm, v_hbm, o_ref, lse_ref,
     q_own, k_own, v_own, k_buf, v_buf, bias,
     in_sem, far_send, far_recv, near_send, near_recv,
 ):
-    _, rows, _ = k_buf.shape
-    count = len(chunks)
+    _, rows, total_width = k_buf.shape
+    width = chunk_heads * HEAD_DIM
+    count = total_width // width
+    ahead = min(AHEAD_ODD, count)
     me = lax.axis_index("ctx")
     odd = lax.rem(me, 2) == 1
     even = jnp.logical_not(odd)
@@ -39,8 +35,7 @@
     bufs = (k_buf, v_buf)
 
     def columns(c):
-        start, size = chunks[c]
-        return pl.ds(start * HEAD_DIM, size * HEAD_DIM)
+        return pl.ds(pl.multiple_of(c * width, width), width)
 
     def far(c, t):
         return pltpu.make_async_remote_copy(
@@ -82,20 +77,30 @@
         for t in range(2):
             far(c, t).start()
 
-    @pl.when(even)
-    def _():
-        for c in range(count):
-            for t in range(2):
-                near(c, t).start()
-
-            @pl.when(has_far_target)
-            def _():
-                start_far(c)
+    def start_near(c):
+        for t in range(2):
+            near(c, t).start()
+
+    def each(start, stop, body):
+        def step(c, carry):
+            body(c)
+            return carry
+        lax.fori_loop(start, stop, step, 0)
+
+    @pl.when(even & has_far_target)
+    def _():
+        def both(c):
+            start_near(c)
+            start_far(c)
+        each(0, count, both)
+
+    @pl.when(even & jnp.logical_not(has_far_target))
+    def _():
+        each(0, count, start_near)
 
     @pl.when(odd & has_far_target)
     def _():
-        for c in range(min(AHEAD_ODD, count)):
-            start_far(c)
+        each(0, ahead, start_far)
 
     for copy in local:
         copy.start()
@@ -120,7 +125,7 @@
     for copy in local:
         copy.wait()
 
-    def head(h, carry):
+    def head(h):
         place = pl.ds(pl.multiple_of(h * HEAD_DIM, HEAD_DIM), HEAD_DIM)
         q = q_own[:, place]
         k = k_buf[:, :, place].reshape((KV_STEPS - 1) * rows, HEAD_DIM)
@@ -140,7 +145,6 @@
         diagonal = (lax.broadcasted_iota(jnp.int32, (rows, rows), 0)
                     == lax.broadcasted_iota(jnp.int32, (rows, rows), 1))
         lse_ref[pl.ds(h, 1), :] = jnp.sum(jnp.where(diagonal, lse, 0.0), axis=0, keepdims=True)
-        return carry
 
     def finish_chunk(c):
         @pl.when(even & has_far_source)
@@ -153,36 +157,40 @@
             for t in range(2):
                 near(c, t).wait_recv()
 
-        start, size = chunks[c]
-        lax.fori_loop(start, start + size, head, 0)
-
-    for c in range(count):
+        for h in range(chunk_heads):
+            head(c * chunk_heads + h)
+
+    def step(c):
         @pl.when(odd & has_far_source)
         def _():
             for t in range(2):
                 far(c, t).wait_recv()
                 relay(c, t).start()
 
-        if c + AHEAD_ODD < count:
-            @pl.when(odd & has_far_target)
-            def _():
-                start_far(c + AHEAD_ODD)
-
-        if c >= 1:
+        @pl.when(odd & has_far_target & (c + ahead < count))
+        def _():
+            start_far(c + ahead)
+
+        @pl.when(c >= 1)
+        def _():
             finish_chunk(c - 1)
+
+    each(0, count, step)
     finish_chunk(count - 1)
 
     @pl.when(has_far_target)
     def _():
-        for c in range(count):
+        def body(c):
             for t in range(2):
                 far(c, t).wait_send()
+        each(0, count, body)
 
     @pl.when(even | has_far_source)
     def _():
-        for c in range(count):
+        def body(c):
             for t in range(2):
                 near(c, t).wait_send()
+        each(0, count, body)
 
 
 def write_kernel(o_vmem, lse_vmem, o_hbm, lse_hbm, sem):
@@ -215,11 +223,11 @@
 def shards(n, att_query, att_key, att_value):
     rows, total_width = att_query.shape
     heads = total_width // HEAD_DIM
-    chunks = chunks_of(heads)
-    count = len(chunks)
+    chunk_heads = math.gcd(heads, CHUNK_HEADS)
+    count = heads // chunk_heads
     bf16 = att_query.dtype
     attn_out, attn_lse = pl.pallas_call(
-        functools.partial(kernel, n, chunks),
+        functools.partial(kernel, n, chunk_heads),
         out_shape=(
             pltpu.VMEM((rows, total_width), bf16),
             pltpu.VMEM((heads, rows), jnp.float32),

time: 57.3 us -> 57 us (level)
  no operation moved by 1% of the time
where the time goes in v5:
time: 57 us; the launch traced here: 56.9 us
  Pallas kernels  56.2 us (99%)
  between operations  0.64 us (1%)
    pallas_call x1, Pallas kernels, shards(): pl.pallas_call(functools.partial(kernel, n, chunk_heads), out_shape=(pltp...  55.2 us

profile of v5, /device:TPU:24, one launch (start us, length us, event | category | flops | bytes accessed | tf_op | source)
XLA Modules:
  0.0 56.9 jit_solution(4427980864614570160)
XLA Ops:
  0.6 55.2 %shard_map.50 = (bf16[128,4096]{1,0:T(8,128)(2,1)S(1)}, f32[32,128]{1,0:T(8,128)S(1)}) custom-call(bf16[128,4096]{1,0:T(8,128)(2,1)} %q_hbm.1, bf16[128,4096]{1,0:T(8,128)(2,1)} %k_hbm.1, bf16[128,4096]{1,0:T(8,128)(2,1)} %v_hbm.1), custom_call_target="tpu_custom_call" | custom-call | flops 805306368 | bytes 4194304 | tf_op jit(solution)/shard_map/pallas_call | solution.py:229
  55.9 1.0 %shard_map.51 = (bf16[128,4096]{1,0:T(8,128)(2,1)}, f32[32,128]{1,0:T(8,128)}) custom-call(bf16[128,4096]{1,0:T(8,128)(2,1)S(1)} %get-tuple-element.4.o_vmem, f32[32,128]{1,0:T(8,128)S(1)} %get-tuple-element.5.lse_vmem), custom_call_target="tpu_custom_call" | custom-call | bytes 2097152 | tf_op jit(solution)/shard_map/pallas_call | solution.py:208

commit v6 on v5

--- a/solution.py
+++ b/solution.py
@@ -10,8 +10,8 @@
 
 HEAD_DIM = 128
 KV_STEPS = 3
-CHUNK_HEADS = 1
-AHEAD_ODD = 5
+CHUNK_HEADS = 2
+AHEAD_ODD = 3
 MESH = pl.DeviceIdType.MESH
 
 

time: 57 us -> 56.5 us (level)
  no operation moved by 1% of the time
where the time goes in v6:
time: 56.5 us; the launch traced here: 56.3 us
  Pallas kernels  55.7 us (99%)
  between operations  0.64 us (1%)
    pallas_call x1, Pallas kernels, shards(): pl.pallas_call(functools.partial(kernel, n, chunk_heads), out_shape=(pltp...  54.7 us

profile of v6, /device:TPU:24, one launch (start us, length us, event | category | flops | bytes accessed | tf_op | source)
XLA Modules:
  0.0 56.3 jit_solution(8839434826525562032)
XLA Ops:
  0.6 54.7 %shard_map.50 = (bf16[128,4096]{1,0:T(8,128)(2,1)S(1)}, f32[32,128]{1,0:T(8,128)S(1)}) custom-call(bf16[128,4096]{1,0:T(8,128)(2,1)} %q_hbm.1, bf16[128,4096]{1,0:T(8,128)(2,1)} %k_hbm.1, bf16[128,4096]{1,0:T(8,128)(2,1)} %v_hbm.1), custom_call_target="tpu_custom_call" | custom-call | flops 805306368 | bytes 4194304 | tf_op jit(solution)/shard_map/pallas_call | solution.py:229
  55.4 1.0 %shard_map.51 = (bf16[128,4096]{1,0:T(8,128)(2,1)}, f32[32,128]{1,0:T(8,128)}) custom-call(bf16[128,4096]{1,0:T(8,128)(2,1)S(1)} %get-tuple-element.4.o_vmem, f32[32,128]{1,0:T(8,128)S(1)} %get-tuple-element.5.lse_vmem), custom_call_target="tpu_custom_call" | custom-call | bytes 2097152 | tf_op jit(solution)/shard_map/pallas_call | solution.py:208

commit v7 on v6

--- a/solution.py
+++ b/solution.py
@@ -12,6 +12,7 @@
 KV_STEPS = 3
 CHUNK_HEADS = 2
 AHEAD_ODD = 3
+LAG = 2
 MESH = pl.DeviceIdType.MESH
 
 
@@ -125,26 +126,12 @@
     for copy in local:
         copy.wait()
 
-    def head(h):
-        place = pl.ds(pl.multiple_of(h * HEAD_DIM, HEAD_DIM), HEAD_DIM)
-        q = q_own[:, place]
-        k = k_buf[:, :, place].reshape((KV_STEPS - 1) * rows, HEAD_DIM)
-        v = v_buf[:, :, place].reshape((KV_STEPS - 1) * rows, HEAD_DIM)
-        s = jnp.concatenate([
-            lax.dot_general(q, block, (((1,), (1,)), ((), ())), preferred_element_type=jnp.float32)
-            for block in (k, k_own[:, place])], axis=1) + bias[...]
-        m = jnp.max(s, axis=1, keepdims=True)
-        w = jnp.exp2((s - m) * factor)
-        total = jnp.sum(w, axis=1, keepdims=True)
-        w = w.astype(jnp.bfloat16)
-        split = (KV_STEPS - 1) * rows
-        mixed = jnp.dot(w[:, :split], v, preferred_element_type=jnp.float32)
-        mixed += jnp.dot(w[:, split:], v_own[:, place], preferred_element_type=jnp.float32)
-        o_ref[:, place] = (mixed / total).astype(o_ref.dtype)
-        lse = m * (1.0 / math.sqrt(HEAD_DIM)) + jnp.log(total)
-        diagonal = (lax.broadcasted_iota(jnp.int32, (rows, rows), 0)
-                    == lax.broadcasted_iota(jnp.int32, (rows, rows), 1))
-        lse_ref[pl.ds(h, 1), :] = jnp.sum(jnp.where(diagonal, lse, 0.0), axis=0, keepdims=True)
+    def scores(q, block, columns_of_bias):
+        return lax.dot_general(
+            q, block, (((1,), (1,)), ((), ())), preferred_element_type=jnp.float32
+        ) + bias[:, columns_of_bias]
+
+    far_place, near_place, own_place = (slice(i * rows, (i + 1) * rows) for i in range(KV_STEPS))
 
     def finish_chunk(c):
         @pl.when(even & has_far_source)
@@ -152,16 +139,60 @@
             for t in range(2):
                 far(c, t).wait_recv()
 
+        places = [
+            pl.ds(pl.multiple_of((c * chunk_heads + h) * HEAD_DIM, HEAD_DIM), HEAD_DIM)
+            for h in range(chunk_heads)
+        ]
+        first = []
+        for place in places:
+            q = q_own[:, place]
+            s_far = scores(q, k_buf[0, :, place], far_place)
+            s_own = scores(q, k_own[:, place], own_place)
+            m = jnp.maximum(jnp.max(s_far, axis=1, keepdims=True), jnp.max(s_own, axis=1, keepdims=True))
+            w_far = jnp.exp2((s_far - m) * factor)
+            w_own = jnp.exp2((s_own - m) * factor)
+            total = jnp.sum(w_far + w_own, axis=1, keepdims=True)
+            mixed = jnp.dot(w_far.astype(jnp.bfloat16), v_buf[0, :, place], preferred_element_type=jnp.float32)
+            mixed += jnp.dot(w_own.astype(jnp.bfloat16), v_own[:, place], preferred_element_type=jnp.float32)
+            first.append((m, total, mixed))
+
         @pl.when(has_near_source)
         def _():
-            for t in range(2):
-                near(c, t).wait_recv()
-
-        for h in range(chunk_heads):
-            head(c * chunk_heads + h)
+            near(c, 0).wait_recv()
+
+        second = []
+        for place, (m_first, total, mixed) in zip(places, first):
+            s = scores(q_own[:, place], k_buf[1, :, place], near_place)
+            m = jnp.maximum(m_first, jnp.max(s, axis=1, keepdims=True))
+            w = jnp.exp2((s - m) * factor)
+            scale = jnp.exp2((m_first - m) * factor)
+            total = total * scale + jnp.sum(w, axis=1, keepdims=True)
+            inverse = 1.0 / total
+            second.append((w.astype(jnp.bfloat16), mixed * (scale * inverse), inverse))
+            lse = m * (1.0 / math.sqrt(HEAD_DIM)) + jnp.log(total)
+            diagonal = (lax.broadcasted_iota(jnp.int32, (rows, rows), 0)
+                        == lax.broadcasted_iota(jnp.int32, (rows, rows), 1))
+            lse_ref[pl.ds(c * chunk_heads + len(second) - 1, 1), :] = jnp.sum(
+                jnp.where(diagonal, lse, 0.0), axis=0, keepdims=True)
+
+        @pl.when(has_near_source)
+        def _():
+            near(c, 1).wait_recv()
+
+        for place, (w, mixed, inverse) in zip(places, second):
+            mixed += jnp.dot(w, v_buf[1, :, place], preferred_element_type=jnp.float32) * inverse
+            o_ref[:, place] = mixed.astype(o_ref.dtype)
+
+    def wait_far_sends(c):
+        for t in range(2):
+            far(c, t).wait_send()
+
+    def wait_near_sends(c):
+        for t in range(2):
+            near(c, t).wait_send()
 
     def step(c):
-        @pl.when(odd & has_far_source)
+        @pl.when(odd & has_far_source & (c < count))
         def _():
             for t in range(2):
                 far(c, t).wait_recv()
@@ -171,26 +202,27 @@
         def _():
             start_far(c + ahead)
 
-        @pl.when(c >= 1)
-        def _():
-            finish_chunk(c - 1)
-
-    each(0, count, step)
-    finish_chunk(count - 1)
-
-    @pl.when(has_far_target)
-    def _():
-        def body(c):
-            for t in range(2):
-                far(c, t).wait_send()
-        each(0, count, body)
-
-    @pl.when(even | has_far_source)
-    def _():
-        def body(c):
-            for t in range(2):
-                near(c, t).wait_send()
-        each(0, count, body)
+        @pl.when(even & (c == count + LAG - 1))
+        def _():
+            each(0, count, wait_near_sends)
+
+            @pl.when(has_far_target)
+            def _():
+                each(0, count, wait_far_sends)
+
+        @pl.when(c >= LAG)
+        def _():
+            finish_chunk(c - LAG)
+
+    each(0, count + LAG, step)
+
+    @pl.when(odd & has_far_target)
+    def _():
+        each(0, count, wait_far_sends)
+
+    @pl.when(odd & has_far_source)
+    def _():
+        each(0, count, wait_near_sends)
 
 
 def write_kernel(o_vmem, lse_vmem, o_hbm, lse_hbm, sem):

time: 56.5 us -> 55.8 us (0.988)
  Pallas kernels: 55.7 us -> 55.1 us
    pallas_call x1, Pallas kernels: 54.7 us -> 54.1 us  [shards(): pl.pallas_call(functools.partial(kernel, n, chunk_heads), out_shape=(pltp...]
where the time goes in v7:
time: 55.8 us; the launch traced here: 55.7 us
  Pallas kernels  55.1 us (99%)
  between operations  0.64 us (1%)
    pallas_call x1, Pallas kernels, shards(): pl.pallas_call(functools.partial(kernel, n, chunk_heads), out_shape=(pltp...  54.1 us

profile of v7, /device:TPU:24, one launch (start us, length us, event | category | flops | bytes accessed | tf_op | source)
XLA Modules:
  0.0 55.7 jit_solution(1707974027469291092)
XLA Ops:
  0.6 54.1 %shard_map.50 = (bf16[128,4096]{1,0:T(8,128)(2,1)S(1)}, f32[32,128]{1,0:T(8,128)S(1)}) custom-call(bf16[128,4096]{1,0:T(8,128)(2,1)} %q_hbm.1, bf16[128,4096]{1,0:T(8,128)(2,1)} %k_hbm.1, bf16[128,4096]{1,0:T(8,128)(2,1)} %v_hbm.1), custom_call_target="tpu_custom_call" | custom-call | flops 805306368 | bytes 4194304 | tf_op jit(solution)/shard_map/pallas_call | solution.py:261
  54.7 1.0 %shard_map.51 = (bf16[128,4096]{1,0:T(8,128)(2,1)}, f32[32,128]{1,0:T(8,128)}) custom-call(bf16[128,4096]{1,0:T(8,128)(2,1)S(1)} %get-tuple-element.4.o_vmem, f32[32,128]{1,0:T(8,128)S(1)} %get-tuple-element.5.lse_vmem), custom_call_target="tpu_custom_call" | custom-call | bytes 2097152 | tf_op jit(solution)/shard_map/pallas_call | solution.py:240

commit v8 on v7

--- a/solution.py
+++ b/solution.py
@@ -12,18 +12,17 @@
 KV_STEPS = 3
 CHUNK_HEADS = 2
 AHEAD_ODD = 3
-LAG = 2
+LAG = 1
 MESH = pl.DeviceIdType.MESH
 
 
 def kernel(
-    n, chunk_heads, q_hbm, k_hbm, v_hbm, o_ref, lse_ref,
+    n, q_hbm, k_hbm, v_hbm, o_ref, lse_ref,
     q_own, k_own, v_own, k_buf, v_buf, bias,
     in_sem, far_send, far_recv, near_send, near_recv,
 ):
-    _, rows, total_width = k_buf.shape
-    width = chunk_heads * HEAD_DIM
-    count = total_width // width
+    count, rows, width = k_own.shape
+    chunk_heads = width // HEAD_DIM
     ahead = min(AHEAD_ODD, count)
     me = lax.axis_index("ctx")
     odd = lax.rem(me, 2) == 1
@@ -32,7 +31,7 @@
     has_far_target = me + 2 < n
     has_far_source = me >= 2
     has_near_source = me >= 1
-    hbm = (k_hbm, v_hbm)
+    own = (k_own, v_own)
     bufs = (k_buf, v_buf)
 
     def columns(c):
@@ -40,47 +39,26 @@
 
     def far(c, t):
         return pltpu.make_async_remote_copy(
-            src_ref=hbm[t].at[:, columns(c)], dst_ref=bufs[t].at[0, :, columns(c)],
+            src_ref=own[t].at[c], dst_ref=bufs[t].at[0, c],
             send_sem=far_send.at[c, t], recv_sem=far_recv.at[c, t],
             device_id={"ctx": lax.rem(me + 2, n)}, device_id_type=MESH)
 
     def near(c, t):
         return pltpu.make_async_remote_copy(
-            src_ref=hbm[t].at[:, columns(c)], dst_ref=bufs[t].at[1, :, columns(c)],
+            src_ref=own[t].at[c], dst_ref=bufs[t].at[1, c],
             send_sem=near_send.at[c, t], recv_sem=near_recv.at[c, t],
             device_id={"ctx": partner}, device_id_type=MESH)
 
     def relay(c, t):
         return pltpu.make_async_remote_copy(
-            src_ref=bufs[t].at[0, :, columns(c)], dst_ref=bufs[t].at[1, :, columns(c)],
+            src_ref=bufs[t].at[0, c], dst_ref=bufs[t].at[1, c],
             send_sem=near_send.at[c, t], recv_sem=near_recv.at[c, t],
             device_id={"ctx": partner}, device_id_type=MESH)
 
-    local = [
-        pltpu.make_async_copy(source, target, in_sem.at[i])
-        for i, (source, target) in enumerate(((q_hbm, q_own), (k_hbm, k_own), (v_hbm, v_own)))
-    ]
-
-    barrier = pltpu.get_barrier_semaphore()
-    pl.semaphore_signal(barrier, inc=1, device_id={"ctx": partner}, device_id_type=MESH)
-
-    @pl.when(has_far_target)
-    def _():
-        pl.semaphore_signal(barrier, inc=1, device_id={"ctx": lax.rem(me + 2, n)}, device_id_type=MESH)
-
-    @pl.when(has_far_source)
-    def _():
-        pl.semaphore_signal(barrier, inc=1, device_id={"ctx": lax.rem(me + n - 2, n)}, device_id_type=MESH)
-
-    pl.semaphore_wait(barrier, 1 + has_far_target.astype(jnp.int32) + has_far_source.astype(jnp.int32))
-
-    def start_far(c):
-        for t in range(2):
-            far(c, t).start()
-
-    def start_near(c):
-        for t in range(2):
-            near(c, t).start()
+    def local(c, t):
+        source = (k_hbm, v_hbm, q_hbm)[t]
+        target = (k_own, v_own, q_own)[t]
+        return pltpu.make_async_copy(source.at[:, columns(c)], target.at[c], in_sem.at[c, t])
 
     def each(start, stop, body):
         def step(c, carry):
@@ -88,23 +66,50 @@
             return carry
         lax.fori_loop(start, stop, step, 0)
 
-    @pl.when(even & has_far_target)
-    def _():
-        def both(c):
+    barrier = pltpu.get_barrier_semaphore()
+    pl.semaphore_signal(barrier, inc=1, device_id={"ctx": partner}, device_id_type=MESH)
+
+    @pl.when(has_far_target)
+    def _():
+        pl.semaphore_signal(barrier, inc=1, device_id={"ctx": lax.rem(me + 2, n)}, device_id_type=MESH)
+
+    @pl.when(has_far_source)
+    def _():
+        pl.semaphore_signal(barrier, inc=1, device_id={"ctx": lax.rem(me + n - 2, n)}, device_id_type=MESH)
+
+    def start_local(c):
+        for t in range(2):
+            local(c, t).start()
+
+    each(0, count, start_local)
+
+    pl.semaphore_wait(barrier, 1 + has_far_target.astype(jnp.int32) + has_far_source.astype(jnp.int32))
+
+    def start_far(c):
+        for t in range(2):
+            far(c, t).start()
+
+    def start_near(c):
+        for t in range(2):
+            near(c, t).start()
+
+    def wait_local(c):
+        for t in range(2):
+            local(c, t).wait()
+
+    def first_sends(c):
+        wait_local(c)
+
+        @pl.when(even)
+        def _():
             start_near(c)
+
+        @pl.when(has_far_target & (even | (c < ahead)))
+        def _():
             start_far(c)
-        each(0, count, both)
-
-    @pl.when(even & jnp.logical_not(has_far_target))
-    def _():
-        each(0, count, start_near)
-
-    @pl.when(odd & has_far_target)
-    def _():
-        each(0, ahead, start_far)
-
-    for copy in local:
-        copy.start()
+
+    each(0, count, first_sends)
+    each(0, count, lambda c: local(c, 2).start())
 
     @pl.when(jnp.logical_not(has_far_source))
     def _():
@@ -123,8 +128,7 @@
     bias[...] = jnp.where(allowed, 0.0, -jnp.inf)
     factor = math.log2(math.e) / math.sqrt(HEAD_DIM)
 
-    for copy in local:
-        copy.wait()
+    each(0, count, lambda c: local(c, 2).wait())
 
     def scores(q, block, columns_of_bias):
         return lax.dot_general(
@@ -139,21 +143,18 @@
             for t in range(2):
                 far(c, t).wait_recv()
 
-        places = [
-            pl.ds(pl.multiple_of((c * chunk_heads + h) * HEAD_DIM, HEAD_DIM), HEAD_DIM)
-            for h in range(chunk_heads)
-        ]
+        places = [slice(h * HEAD_DIM, (h + 1) * HEAD_DIM) for h in range(chunk_heads)]
         first = []
         for place in places:
-            q = q_own[:, place]
-            s_far = scores(q, k_buf[0, :, place], far_place)
-            s_own = scores(q, k_own[:, place], own_place)
+            q = q_own[c, :, place]
+            s_far = scores(q, k_buf[0, c, :, place], far_place)
+            s_own = scores(q, k_own[c, :, place], own_place)
             m = jnp.maximum(jnp.max(s_far, axis=1, keepdims=True), jnp.max(s_own, axis=1, keepdims=True))
             w_far = jnp.exp2((s_far - m) * factor)
             w_own = jnp.exp2((s_own - m) * factor)
             total = jnp.sum(w_far + w_own, axis=1, keepdims=True)
-            mixed = jnp.dot(w_far.astype(jnp.bfloat16), v_buf[0, :, place], preferred_element_type=jnp.float32)
-            mixed += jnp.dot(w_own.astype(jnp.bfloat16), v_own[:, place], preferred_element_type=jnp.float32)
+            mixed = jnp.dot(w_far.astype(jnp.bfloat16), v_buf[0, c, :, place], preferred_element_type=jnp.float32)
+            mixed += jnp.dot(w_own.astype(jnp.bfloat16), v_own[c, :, place], preferred_element_type=jnp.float32)
             first.append((m, total, mixed))
 
         @pl.when(has_near_source)
@@ -162,7 +163,7 @@
 
         second = []
         for place, (m_first, total, mixed) in zip(places, first):
-            s = scores(q_own[:, place], k_buf[1, :, place], near_place)
+            s = scores(q_own[c, :, place], k_buf[1, c, :, place], near_place)
             m = jnp.maximum(m_first, jnp.max(s, axis=1, keepdims=True))
             w = jnp.exp2((s - m) * factor)
             scale = jnp.exp2((m_first - m) * factor)
@@ -179,8 +180,9 @@
         def _():
             near(c, 1).wait_recv()
 
-        for place, (w, mixed, inverse) in zip(places, second):
-            mixed += jnp.dot(w, v_buf[1, :, place], preferred_element_type=jnp.float32) * inverse
+        for h, (w, mixed, inverse) in enumerate(second):
+            mixed += jnp.dot(w, v_buf[1, c, :, places[h]], preferred_element_type=jnp.float32) * inverse
+            place = pl.ds(pl.multiple_of((c * chunk_heads + h) * HEAD_DIM, HEAD_DIM), HEAD_DIM)
             o_ref[:, place] = mixed.astype(o_ref.dtype)
 
     def wait_far_sends(c):
@@ -202,27 +204,25 @@
         def _():
             start_far(c + ahead)
 
-        @pl.when(even & (c == count + LAG - 1))
-        def _():
-            each(0, count, wait_near_sends)
-
+        @pl.when(c == count + LAG - 1)
+        def _():
             @pl.when(has_far_target)
             def _():
                 each(0, count, wait_far_sends)
 
+            @pl.when(even | has_far_source)
+            def _():
+                each(0, count - 2, wait_near_sends)
+
         @pl.when(c >= LAG)
         def _():
             finish_chunk(c - LAG)
 
     each(0, count + LAG, step)
 
-    @pl.when(odd & has_far_target)
-    def _():
-        each(0, count, wait_far_sends)
-
-    @pl.when(odd & has_far_source)
-    def _():
-        each(0, count, wait_near_sends)
+    @pl.when(even | has_far_source)
+    def _():
+        each(count - 2, count, wait_near_sends)
 
 
 def write_kernel(o_vmem, lse_vmem, o_hbm, lse_hbm, sem):
@@ -257,9 +257,10 @@
     heads = total_width // HEAD_DIM
     chunk_heads = math.gcd(heads, CHUNK_HEADS)
     count = heads // chunk_heads
+    width = chunk_heads * HEAD_DIM
     bf16 = att_query.dtype
     attn_out, attn_lse = pl.pallas_call(
-        functools.partial(kernel, n, chunk_heads),
+        functools.partial(kernel, n),
         out_shape=(
             pltpu.VMEM((rows, total_width), bf16),
             pltpu.VMEM((heads, rows), jnp.float32),
@@ -267,13 +268,13 @@
         in_specs=[pl.BlockSpec(memory_space=pltpu.HBM)] * 3,
         out_specs=(pl.BlockSpec(memory_space=pltpu.VMEM), pl.BlockSpec(memory_space=pltpu.VMEM)),
         scratch_shapes=[
-            pltpu.VMEM((rows, total_width), bf16),
-            pltpu.VMEM((rows, total_width), bf16),
-            pltpu.VMEM((rows, total_width), bf16),
-            pltpu.VMEM((KV_STEPS - 1, rows, total_width), bf16),
-            pltpu.VMEM((KV_STEPS - 1, rows, total_width), bf16),
+            pltpu.VMEM((count, rows, width), bf16),
+            pltpu.VMEM((count, rows, width), bf16),
+            pltpu.VMEM((count, rows, width), bf16),
+            pltpu.VMEM((KV_STEPS - 1, count, rows, width), bf16),
+            pltpu.VMEM((KV_STEPS - 1, count, rows, width), bf16),
             pltpu.VMEM((rows, KV_STEPS * rows), jnp.float32),
-            pltpu.SemaphoreType.DMA((3,)),
+            pltpu.SemaphoreType.DMA((count, 3)),
             pltpu.SemaphoreType.DMA((count, 2)),
             pltpu.SemaphoreType.DMA((count, 2)),
             pltpu.SemaphoreType.DMA((count, 2)),

time: 55.8 us -> 56.1 us (level)
  no operation moved by 1% of the time
where the time goes in v8:
time: 56.1 us; the launch traced here: 55.9 us
  Pallas kernels  55.2 us (98%)
  between operations  0.64 us (1%)
    pallas_call x1, Pallas kernels, shards(): pl.pallas_call(functools.partial(kernel, n), out_shape=(pltpu.VMEM((rows,...  54.2 us

profile of v8, /device:TPU:24, one launch (start us, length us, event | category | flops | bytes accessed | tf_op | source)
XLA Modules:
  0.0 55.9 jit_solution(8144974112825820321)
XLA Ops:
  0.6 54.2 %shard_map.50 = (bf16[128,4096]{1,0:T(8,128)(2,1)S(1)}, f32[32,128]{1,0:T(8,128)S(1)}) custom-call(bf16[128,4096]{1,0:T(8,128)(2,1)} %q_hbm.1, bf16[128,4096]{1,0:T(8,128)(2,1)} %k_hbm.1, bf16[128,4096]{1,0:T(8,128)(2,1)} %v_hbm.1), custom_call_target="tpu_custom_call" | custom-call | flops 805306368 | bytes 4194304 | tf_op jit(solution)/shard_map/pallas_call | solution.py:262
  54.9 1.0 %shard_map.51 = (bf16[128,4096]{1,0:T(8,128)(2,1)}, f32[32,128]{1,0:T(8,128)}) custom-call(bf16[128,4096]{1,0:T(8,128)(2,1)S(1)} %get-tuple-element.4.o_vmem, f32[32,128]{1,0:T(8,128)S(1)} %get-tuple-element.5.lse_vmem), custom_call_target="tpu_custom_call" | custom-call | bytes 2097152 | tf_op jit(solution)/shard_map/pallas_call | solution.py:240

commit v9 on v8

--- a/solution.py
+++ b/solution.py
@@ -19,7 +19,7 @@
 def kernel(
     n, q_hbm, k_hbm, v_hbm, o_ref, lse_ref,
     q_own, k_own, v_own, k_buf, v_buf, bias,
-    in_sem, far_send, far_recv, near_send, near_recv,
+    in_sem, far_send, far_recv, near_send, near_recv, direct_send,
 ):
     count, rows, width = k_own.shape
     chunk_heads = width // HEAD_DIM
@@ -31,6 +31,8 @@
     has_far_target = me + 2 < n
     has_far_source = me >= 2
     has_near_source = me >= 1
+    has_direct_target = odd & (me + 1 < n)
+    has_direct_source = even & (me >= 1)
     own = (k_own, v_own)
     bufs = (k_buf, v_buf)
 
@@ -55,6 +57,12 @@
             send_sem=near_send.at[c, t], recv_sem=near_recv.at[c, t],
             device_id={"ctx": partner}, device_id_type=MESH)
 
+    def direct():
+        return pltpu.make_async_remote_copy(
+            src_ref=own[0].at[0], dst_ref=bufs[0].at[1, 0],
+            send_sem=direct_send.at[0], recv_sem=near_recv.at[0, 0],
+            device_id={"ctx": lax.rem(me + 1, n)}, device_id_type=MESH)
+
     def local(c, t):
         source = (k_hbm, v_hbm, q_hbm)[t]
         target = (k_own, v_own, q_own)[t]
@@ -77,13 +85,22 @@
     def _():
         pl.semaphore_signal(barrier, inc=1, device_id={"ctx": lax.rem(me + n - 2, n)}, device_id_type=MESH)
 
+    @pl.when(has_direct_target)
+    def _():
+        pl.semaphore_signal(barrier, inc=1, device_id={"ctx": lax.rem(me + 1, n)}, device_id_type=MESH)
+
+    @pl.when(has_direct_source)
+    def _():
+        pl.semaphore_signal(barrier, inc=1, device_id={"ctx": lax.rem(me + n - 1, n)}, device_id_type=MESH)
+
     def start_local(c):
         for t in range(2):
             local(c, t).start()
 
     each(0, count, start_local)
 
-    pl.semaphore_wait(barrier, 1 + has_far_target.astype(jnp.int32) + has_far_source.astype(jnp.int32))
+    peers = (has_far_target, has_far_source, has_direct_target, has_direct_source)
+    pl.semaphore_wait(barrier, 1 + sum(peer.astype(jnp.int32) for peer in peers))
 
     def start_far(c):
         for t in range(2):
@@ -107,6 +124,10 @@
         @pl.when(has_far_target & (even | (c < ahead)))
         def _():
             start_far(c)
+
+        @pl.when(has_direct_target & (c == 0))
+        def _():
+            direct().start()
 
     each(0, count, first_sends)
     each(0, count, lambda c: local(c, 2).start())
@@ -190,15 +211,23 @@
             far(c, t).wait_send()
 
     def wait_near_sends(c):
-        for t in range(2):
-            near(c, t).wait_send()
+        @pl.when(even | (c > 0))
+        def _():
+            near(c, 0).wait_send()
+
+        near(c, 1).wait_send()
 
     def step(c):
         @pl.when(odd & has_far_source & (c < count))
         def _():
-            for t in range(2):
-                far(c, t).wait_recv()
-                relay(c, t).start()
+            far(c, 0).wait_recv()
+
+            @pl.when(c > 0)
+            def _():
+                relay(c, 0).start()
+
+            far(c, 1).wait_recv()
+            relay(c, 1).start()
 
         @pl.when(odd & has_far_target & (c + ahead < count))
         def _():
@@ -223,6 +252,10 @@
     @pl.when(even | has_far_source)
     def _():
         each(count - 2, count, wait_near_sends)
+
+    @pl.when(has_direct_target)
+    def _():
+        direct().wait_send()
 
 
 def write_kernel(o_vmem, lse_vmem, o_hbm, lse_hbm, sem):
@@ -279,6 +312,7 @@
             pltpu.SemaphoreType.DMA((count, 2)),
             pltpu.SemaphoreType.DMA((count, 2)),
             pltpu.SemaphoreType.DMA((count, 2)),
+            pltpu.SemaphoreType.DMA((1,)),
         ],
         compiler_params=pltpu.CompilerParams(
             collective_id=0, has_side_effects=True, vmem_limit_bytes=32 * 1024 * 1024),

time: 56.1 us -> 57.5 us (1.025)
  Pallas kernels: 55.2 us -> 56.6 us
    pallas_call x1, Pallas kernels: 54.2 us -> 55.6 us  [shards(): pl.pallas_call(functools.partial(kernel, n), out_shape=(pltpu.VMEM((rows,...]
where the time goes in v9:
time: 57.5 us; the launch traced here: 57.3 us
  Pallas kernels  56.6 us (98%)
  between operations  0.64 us (1%)
    pallas_call x1, Pallas kernels, shards(): pl.pallas_call(functools.partial(kernel, n), out_shape=(pltpu.VMEM((rows,...  55.6 us

profile of v9, /device:TPU:24, one launch (start us, length us, event | category | flops | bytes accessed | tf_op | source)
XLA Modules:
  0.0 57.3 jit_solution(1507706462719436984)
XLA Ops:
  0.6 55.6 %shard_map.50 = (bf16[128,4096]{1,0:T(8,128)(2,1)S(1)}, f32[32,128]{1,0:T(8,128)S(1)}) custom-call(bf16[128,4096]{1,0:T(8,128)(2,1)} %q_hbm.1, bf16[128,4096]{1,0:T(8,128)(2,1)} %k_hbm.1, bf16[128,4096]{1,0:T(8,128)(2,1)} %v_hbm.1), custom_call_target="tpu_custom_call" | custom-call | flops 805306368 | bytes 4194304 | tf_op jit(solution)/shard_map/pallas_call | solution.py:295
  56.3 1.0 %shard_map.51 = (bf16[128,4096]{1,0:T(8,128)(2,1)}, f32[32,128]{1,0:T(8,128)}) custom-call(bf16[128,4096]{1,0:T(8,128)(2,1)S(1)} %get-tuple-element.4.o_vmem, f32[32,128]{1,0:T(8,128)S(1)} %get-tuple-element.5.lse_vmem), custom_call_target="tpu_custom_call" | custom-call | bytes 2097152 | tf_op jit(solution)/shard_map/pallas_call | solution.py:273

commit v10 on v8

--- a/solution.py
+++ b/solution.py
@@ -10,8 +10,8 @@
 
 HEAD_DIM = 128
 KV_STEPS = 3
-CHUNK_HEADS = 2
-AHEAD_ODD = 3
+CHUNK_HEADS = 1
+AHEAD_ODD = 5
 LAG = 1
 MESH = pl.DeviceIdType.MESH
 

time: 56.1 us -> 58.1 us (1.036)
  Pallas kernels: 55.2 us -> 57.1 us
    pallas_call x1, Pallas kernels: 54.2 us -> 56.2 us  [shards(): pl.pallas_call(functools.partial(kernel, n), out_shape=(pltpu.VMEM((rows,...]
where the time goes in v10:
time: 58.1 us; the launch traced here: 57.8 us
  Pallas kernels  57.1 us (98%)
  between operations  0.64 us (1%)
    pallas_call x1, Pallas kernels, shards(): pl.pallas_call(functools.partial(kernel, n), out_shape=(pltpu.VMEM((rows,...  56.2 us

profile of v10, /device:TPU:24, one launch (start us, length us, event | category | flops | bytes accessed | tf_op | source)
XLA Modules:
  0.0 57.8 jit_solution(838417026243908561)
XLA Ops:
  0.6 56.2 %shard_map.50 = (bf16[128,4096]{1,0:T(8,128)(2,1)S(1)}, f32[32,128]{1,0:T(8,128)S(1)}) custom-call(bf16[128,4096]{1,0:T(8,128)(2,1)} %q_hbm.1, bf16[128,4096]{1,0:T(8,128)(2,1)} %k_hbm.1, bf16[128,4096]{1,0:T(8,128)(2,1)} %v_hbm.1), custom_call_target="tpu_custom_call" | custom-call | flops 805306368 | bytes 4194304 | tf_op jit(solution)/shard_map/pallas_call | solution.py:262
  56.8 1.0 %shard_map.51 = (bf16[128,4096]{1,0:T(8,128)(2,1)}, f32[32,128]{1,0:T(8,128)}) custom-call(bf16[128,4096]{1,0:T(8,128)(2,1)S(1)} %get-tuple-element.4.o_vmem, f32[32,128]{1,0:T(8,128)S(1)} %get-tuple-element.5.lse_vmem), custom_call_target="tpu_custom_call" | custom-call | bytes 2097152 | tf_op jit(solution)/shard_map/pallas_call | solution.py:240

commit v11 on v8

--- a/solution.py
+++ b/solution.py
@@ -13,6 +13,7 @@
 CHUNK_HEADS = 2
 AHEAD_ODD = 3
 LAG = 1
+WRITES = 4
 MESH = pl.DeviceIdType.MESH
 
 
@@ -204,7 +205,7 @@
         def _():
             start_far(c + ahead)
 
-        @pl.when(c == count + LAG - 1)
+        @pl.when(c == max(count + LAG - 2, 0))
         def _():
             @pl.when(has_far_target)
             def _():
@@ -226,10 +227,12 @@
 
 
 def write_kernel(o_vmem, lse_vmem, o_hbm, lse_hbm, sem):
+    part = o_vmem.shape[0] // WRITES
     copies = [
-        pltpu.make_async_copy(o_vmem, o_hbm, sem.at[0]),
-        pltpu.make_async_copy(lse_vmem, lse_hbm, sem.at[1]),
-    ]
+        pltpu.make_async_copy(
+            o_vmem.at[pl.ds(i * part, part)], o_hbm.at[pl.ds(i * part, part)], sem.at[i])
+        for i in range(WRITES)
+    ] + [pltpu.make_async_copy(lse_vmem, lse_hbm, sem.at[WRITES])]
     for copy in copies:
         copy.start()
     for copy in copies:
@@ -245,7 +248,7 @@
         ),
         in_specs=[pl.BlockSpec(memory_space=pltpu.VMEM)] * 2,
         out_specs=(pl.BlockSpec(memory_space=pltpu.HBM),) * 2,
-        scratch_shapes=[pltpu.SemaphoreType.DMA((2,))],
+        scratch_shapes=[pltpu.SemaphoreType.DMA((WRITES + 1,))],
         compiler_params=pltpu.CompilerParams(vmem_limit_bytes=32 * 1024 * 1024),
         cost_estimate=pl.CostEstimate(
             flops=0, bytes_accessed=4 * attn_out.size, transcendentals=0),

time: 56.1 us -> 56 us (level)
  no operation moved by 1% of the time
where the time goes in v11:
time: 56 us; the launch traced here: 55.8 us
  Pallas kernels  55.2 us (99%)
  between operations  0.64 us (1%)
    pallas_call x1, Pallas kernels, shards(): pl.pallas_call(functools.partial(kernel, n), out_shape=(pltpu.VMEM((rows,...  54.2 us

profile of v11, /device:TPU:24, one launch (start us, length us, event | category | flops | bytes accessed | tf_op | source)
XLA Modules:
  0.0 55.8 jit_solution(7685138769924474203)
XLA Ops:
  0.6 54.2 %shard_map.50 = (bf16[128,4096]{1,0:T(8,128)(2,1)S(1)}, f32[32,128]{1,0:T(8,128)S(1)}) custom-call(bf16[128,4096]{1,0:T(8,128)(2,1)} %q_hbm.1, bf16[128,4096]{1,0:T(8,128)(2,1)} %k_hbm.1, bf16[128,4096]{1,0:T(8,128)(2,1)} %v_hbm.1), custom_call_target="tpu_custom_call" | custom-call | flops 805306368 | bytes 4194304 | tf_op jit(solution)/shard_map/pallas_call | solution.py:265
  54.8 1.0 %shard_map.51 = (bf16[128,4096]{1,0:T(8,128)(2,1)}, f32[32,128]{1,0:T(8,128)}) custom-call(bf16[128,4096]{1,0:T(8,128)(2,1)S(1)} %get-tuple-element.4.o_vmem, f32[32,128]{1,0:T(8,128)S(1)} %get-tuple-element.5.lse_vmem), custom_call_target="tpu_custom_call" | custom-call | bytes 2097152 | tf_op jit(solution)/shard_map/pallas_call | solution.py:243

commit v12 on v8

--- a/solution.py
+++ b/solution.py
@@ -11,7 +11,7 @@
 HEAD_DIM = 128
 KV_STEPS = 3
 CHUNK_HEADS = 2
-AHEAD_ODD = 3
+AHEAD_ODD = 2
 LAG = 1
 MESH = pl.DeviceIdType.MESH
 

time: 56.1 us -> 56.1 us (level)
  no operation moved by 1% of the time
where the time goes in v12:
time: 56.1 us; the launch traced here: 55.9 us
  Pallas kernels  55.2 us (98%)
  between operations  0.64 us (1%)
    pallas_call x1, Pallas kernels, shards(): pl.pallas_call(functools.partial(kernel, n), out_shape=(pltpu.VMEM((rows,...  54.2 us

profile of v12, /device:TPU:24, one launch (start us, length us, event | category | flops | bytes accessed | tf_op | source)
XLA Modules:
  0.0 55.9 jit_solution(7488215815722241259)
XLA Ops:
  0.6 54.2 %shard_map.50 = (bf16[128,4096]{1,0:T(8,128)(2,1)S(1)}, f32[32,128]{1,0:T(8,128)S(1)}) custom-call(bf16[128,4096]{1,0:T(8,128)(2,1)} %q_hbm.1, bf16[128,4096]{1,0:T(8,128)(2,1)} %k_hbm.1, bf16[128,4096]{1,0:T(8,128)(2,1)} %v_hbm.1), custom_call_target="tpu_custom_call" | custom-call | flops 805306368 | bytes 4194304 | tf_op jit(solution)/shard_map/pallas_call | solution.py:262
  54.9 1.0 %shard_map.51 = (bf16[128,4096]{1,0:T(8,128)(2,1)}, f32[32,128]{1,0:T(8,128)}) custom-call(bf16[128,4096]{1,0:T(8,128)(2,1)S(1)} %get-tuple-element.4.o_vmem, f32[32,128]{1,0:T(8,128)S(1)} %get-tuple-element.5.lse_vmem), custom_call_target="tpu_custom_call" | custom-call | bytes 2097152 | tf_op jit(solution)/shard_map/pallas_call | solution.py:240

commit v13 on v8

--- a/solution.py
+++ b/solution.py
@@ -78,7 +78,7 @@
         pl.semaphore_signal(barrier, inc=1, device_id={"ctx": lax.rem(me + n - 2, n)}, device_id_type=MESH)
 
     def start_local(c):
-        for t in range(2):
+        for t in range(3):
             local(c, t).start()
 
     each(0, count, start_local)
@@ -109,7 +109,6 @@
             start_far(c)
 
     each(0, count, first_sends)
-    each(0, count, lambda c: local(c, 2).start())
 
     @pl.when(jnp.logical_not(has_far_source))
     def _():
@@ -128,8 +127,6 @@
     bias[...] = jnp.where(allowed, 0.0, -jnp.inf)
     factor = math.log2(math.e) / math.sqrt(HEAD_DIM)
 
-    each(0, count, lambda c: local(c, 2).wait())
-
     def scores(q, block, columns_of_bias):
         return lax.dot_general(
             q, block, (((1,), (1,)), ((), ())), preferred_element_type=jnp.float32
@@ -138,6 +135,8 @@
     far_place, near_place, own_place = (slice(i * rows, (i + 1) * rows) for i in range(KV_STEPS))
 
     def finish_chunk(c):
+        local(c, 2).wait()
+
         @pl.when(even & has_far_source)
         def _():
             for t in range(2):

time: 56.1 us -> 56 us (level)
  no operation moved by 1% of the time
where the time goes in v13:
time: 56 us; the launch traced here: 55.9 us
  Pallas kernels  55.2 us (99%)
  between operations  0.64 us (1%)
    pallas_call x1, Pallas kernels, shards(): pl.pallas_call(functools.partial(kernel, n), out_shape=(pltpu.VMEM((rows,...  54.2 us

profile of v13, /device:TPU:24, one launch (start us, length us, event | category | flops | bytes accessed | tf_op | source)
XLA Modules:
  0.0 55.9 jit_solution(61100449688364135)
XLA Ops:
  0.6 54.2 %shard_map.50 = (bf16[128,4096]{1,0:T(8,128)(2,1)S(1)}, f32[32,128]{1,0:T(8,128)S(1)}) custom-call(bf16[128,4096]{1,0:T(8,128)(2,1)} %q_hbm.1, bf16[128,4096]{1,0:T(8,128)(2,1)} %k_hbm.1, bf16[128,4096]{1,0:T(8,128)(2,1)} %v_hbm.1), custom_call_target="tpu_custom_call" | custom-call | flops 805306368 | bytes 4194304 | tf_op jit(solution)/shard_map/pallas_call | solution.py:261
  54.9 1.0 %shard_map.51 = (bf16[128,4096]{1,0:T(8,128)(2,1)}, f32[32,128]{1,0:T(8,128)}) custom-call(bf16[128,4096]{1,0:T(8,128)(2,1)S(1)} %get-tuple-element.4.o_vmem, f32[32,128]{1,0:T(8,128)S(1)} %get-tuple-element.5.lse_vmem), custom_call_target="tpu_custom_call" | custom-call | bytes 2097152 | tf_op jit(solution)/shard_map/pallas_call | solution.py:239
